TPU v7x, 256 devices: a whole 4x4x8 slice. The times are simulated.
256 devices in a mesh: dp: 32 (over z, y), tensor: 8 (over x, core).
Axes of the slice: x: 4, y: 4, z: 8, core: 2. Of those that a mesh axis runs over, the one named last changes fastest.
Arguments:
- x_in: bfloat16 [8192, 16384], P('dp', 'tensor'), may hold values from -125 to 125, as said below
- grad_up: bfloat16 [8192, 53248], P('dp', 'tensor'), may hold values from -125 to 125, as said below
- hidden_act: bfloat16 [8192, 53248], P('dp', 'tensor'), may hold values from -125 to 125, as said below
- grad_down: bfloat16 [8192, 16384], P('dp', 'tensor'), may hold values from -125 to 125, as said below
- sketch_up: bfloat16 [32, 53248], P(None, 'tensor'), may hold values from -4 to 4
- sketch_down: bfloat16 [32, 16384], P(None, 'tensor'), may hold values from -4 to 4
Outputs:
- up_a: float32 [32, 16384], P(None, 'tensor')
- up_b: float32 [32, 53248], P(None, 'tensor')
- down_a: float32 [32, 53248], P(None, 'tensor')
- down_b: float32 [32, 16384], P(None, 'tensor')
Inputs may be any that keep to these rules, and one draw needn't show every extreme that they name: `x_in`: Real-valued entries of order one to some tens; row and column scales vary. `grad_up`: Real-valued entries of order one to some tens; row and column scales vary. `hidden_act`: Real-valued entries of order one to some tens; row and column scales vary. `grad_down`: Real-valued entries of order one to some tens; row and column scales vary.
All inputs are finite; a program needn't handle non-finite values.
Results may differ from a plain program's by a relative error of at most 0.014.
Values may be sent and summed in bfloat16 or wider, within the bound.
A program may use at most 64 MiB of HBM per device.

v0:
```python
import math

import jax
import jax.numpy as jnp
from jax import lax
from jax.sharding import PartitionSpec as P

ITERS = 2


def contract(panel, rows):
    return lax.dot_general(
        panel, rows, (((1,), (1,)), ((), ())), preferred_element_type=jnp.float32
    )


def self_gram(panel):
    return lax.dot_general(
        panel,
        panel,
        (((1,), (1,)), ((), ())),
        precision=lax.Precision.HIGHEST,
        preferred_element_type=jnp.float32,
    )


def normalize_rows(panel, gram):
    lower = jnp.linalg.cholesky(gram)
    return jax.scipy.linalg.solve_triangular(lower, panel, lower=True).astype(jnp.bfloat16)


def sketch_round(left_one, right_one, panel_one, left_two, right_two, panel_two):
    first = contract(panel_one, right_one)
    second = contract(panel_two, right_two)
    first, second = lax.psum((first, second), "tensor")
    result_one = jnp.dot(first.astype(jnp.bfloat16), left_one, preferred_element_type=jnp.float32)
    result_two = jnp.dot(second.astype(jnp.bfloat16), left_two, preferred_element_type=jnp.float32)
    return (result_one, result_two)


def orthonormal_pair(result_one, result_two):
    full_one, full_two = lax.psum((result_one, result_two), "dp")
    gram_one, gram_two = lax.psum((self_gram(full_one), self_gram(full_two)), "tensor")
    return (normalize_rows(full_one, gram_one), normalize_rows(full_two, gram_two))


def local(x_in, grad_up, hidden_act, grad_down, sketch_up, sketch_down):
    up_q, down_q = orthonormal_pair(
        *sketch_round(x_in, grad_up, sketch_up, hidden_act, grad_down, sketch_down)
    )
    for step in range(ITERS):
        up_p, down_p = orthonormal_pair(
            *sketch_round(grad_up, x_in, up_q, grad_down, hidden_act, down_q)
        )
        up_q, down_q = orthonormal_pair(
            *sketch_round(x_in, grad_up, up_p, hidden_act, grad_down, down_p)
        )
    up_image, down_image = sketch_round(grad_up, x_in, up_q, grad_down, hidden_act, down_q)
    up_image, down_image = lax.psum((up_image, down_image), "dp")
    token_total = x_in.shape[0] * lax.axis_size("dp")
    model_width = x_in.shape[1] * lax.axis_size("tensor")
    hidden_width = grad_up.shape[1] * lax.axis_size("tensor")
    scale = 1.0 / math.sqrt(token_total)
    up_a = up_q.astype(jnp.float32) * math.sqrt(model_width)
    down_a = down_q.astype(jnp.float32) * math.sqrt(hidden_width)
    return (up_a, up_image * scale, down_a, down_image * scale)


def solution(mesh):
    in_specs = (
        P("dp", "tensor"),
        P("dp", "tensor"),
        P("dp", "tensor"),
        P("dp", "tensor"),
        P(None, "tensor"),
        P(None, "tensor"),
    )
    out_specs = (P(None, "tensor"), P(None, "tensor"), P(None, "tensor"), P(None, "tensor"))
    return jax.shard_map(local, mesh=mesh, in_specs=in_specs, out_specs=out_specs, check_vma=False)
```

profile of v0, /device:TPU:2, one launch (start us, length us, event | category | flops | bytes accessed | tf_op | source)
XLA Modules:
  0.0 1311.5 jit_solution(13648404188805284453)
XLA Ops:
  7.2 3.3 fusion.62
  11.0 23.1 %all-reduce.16 = (bf16[32,256]{1,0:T(8,128)(2,1)S(1)}, bf16[32,256]{1,0:T(8,128)(2,1)S(1)}) all-reduce(f32[32,256]{1,0:T(8,128)S(1)} %fusion.62, f32[32,256]{1,0:T(8,128)S(1)} %fusion.73), channel_id=1, replica_groups=mesh['dp'=32,'tensor'=8] {'tensor'}, use_global_device_ids=true, to_apply=%region_0.0 | all-reduce | flops 16384 | bytes 98304 | tf_op jit(solution)/shard_map/psum | solution.py:35
  38.0 153.6 %all-reduce.34.cloned.1.call-done = (f32[32,2048]{1,0:T(8,128)}, f32[32,6656]{1,0:T(8,128)}) async-done(((f32[32,2048]{1,0:T(8,128)}, f32[32,6656]{1,0:T(8,128)}), (f32[32,2048]{1,0:T(8,128)}, f32[32,6656]{1,0:T(8,128)})) %all-reduce.34.cloned.1.call-update) | async-done | bytes 1114128 | tf_op jit(solution)/shard_map/psum | solution.py:42
  193.0 2.2 fusion.74
  195.2 20.7 %all-reduce.15 = (f32[32,32]{0,1:T(8,128)S(1)}, f32[32,32]{0,1:T(8,128)S(1)}) all-reduce(f32[32,32]{0,1:T(8,128)S(1)} %fusion.63, f32[32,32]{0,1:T(8,128)S(1)} %fusion.74), channel_id=1, replica_groups=mesh['dp'=32,'tensor'=8] {'tensor'}, use_global_device_ids=true, to_apply=%region_2.0 | all-reduce | flops 2048 | bytes 16384 | tf_op jit(solution)/shard_map/psum | solution.py:43
  216.1 2.9 cholesky.219
  220.4 2.4 custom-call.21
  225.9 2.9 cholesky.164
  230.2 2.4 custom-call.16
  235.7 23.9 %all-reduce.14 = (bf16[32,256]{1,0:T(8,128)(2,1)S(1)}, bf16[32,256]{1,0:T(8,128)(2,1)S(1)}) all-reduce(f32[32,256]{1,0:T(8,128)S(1)} %fusion.64, f32[32,256]{1,0:T(8,128)S(1)} %fusion.75), channel_id=1, replica_groups=mesh['dp'=32,'tensor'=8] {'tensor'}, use_global_device_ids=true, to_apply=%region_5.8 | all-reduce | flops 16384 | bytes 98304 | tf_op jit(solution)/shard_map/psum | solution.py:35
  261.8 3.6 fusion.94
  265.5 147.7 %all-reduce.32.cloned.1.call-done = (f32[32,6656]{1,0:T(8,128)}, f32[32,2048]{1,0:T(8,128)}) async-done(((f32[32,6656]{1,0:T(8,128)}, f32[32,2048]{1,0:T(8,128)}), (f32[32,6656]{1,0:T(8,128)}, f32[32,2048]{1,0:T(8,128)})) %all-reduce.32.cloned.1.call-update) | async-done | bytes 1114128 | tf_op jit(solution)/shard_map/psum | solution.py:42
  413.1 2.2 fusion.65
  416.8 20.7 %all-reduce.13 = (f32[32,32]{0,1:T(8,128)S(1)}, f32[32,32]{0,1:T(8,128)S(1)}) all-reduce(f32[32,32]{0,1:T(8,128)S(1)} %fusion.65, f32[32,32]{0,1:T(8,128)S(1)} %fusion.76), channel_id=1, replica_groups=mesh['dp'=32,'tensor'=8] {'tensor'}, use_global_device_ids=true, to_apply=%region_7.10 | all-reduce | flops 2048 | bytes 16384 | tf_op jit(solution)/shard_map/psum | solution.py:43
  437.6 2.9 cholesky.175
  441.8 2.4 custom-call.17
  446.3 3.0 fusion.66
  449.4 2.9 cholesky.230
  453.7 2.4 custom-call.22
  459.2 24.1 %all-reduce.12 = (bf16[32,256]{1,0:T(8,128)(2,1)S(1)}, bf16[32,256]{1,0:T(8,128)(2,1)S(1)}) all-reduce(f32[32,256]{1,0:T(8,128)S(1)} %fusion.66, f32[32,256]{1,0:T(8,128)S(1)} %fusion.77), channel_id=1, replica_groups=mesh['dp'=32,'tensor'=8] {'tensor'}, use_global_device_ids=true, to_apply=%region_8.0 | all-reduce | flops 16384 | bytes 98304 | tf_op jit(solution)/shard_map/psum | solution.py:35
  487.2 147.7 %all-reduce.30.cloned.1.call-done = (f32[32,2048]{1,0:T(8,128)}, f32[32,6656]{1,0:T(8,128)}) async-done(((f32[32,2048]{1,0:T(8,128)}, f32[32,6656]{1,0:T(8,128)}), (f32[32,2048]{1,0:T(8,128)}, f32[32,6656]{1,0:T(8,128)})) %all-reduce.30.cloned.1.call-update) | async-done | bytes 1114128 | tf_op jit(solution)/shard_map/psum | solution.py:42
  636.2 2.2 fusion.78
  638.5 20.7 %all-reduce.11 = (f32[32,32]{0,1:T(8,128)S(1)}, f32[32,32]{0,1:T(8,128)S(1)}) all-reduce(f32[32,32]{0,1:T(8,128)S(1)} %fusion.67, f32[32,32]{0,1:T(8,128)S(1)} %fusion.78), channel_id=1, replica_groups=mesh['dp'=32,'tensor'=8] {'tensor'}, use_global_device_ids=true, to_apply=%region_10.0 | all-reduce | flops 2048 | bytes 16384 | tf_op jit(solution)/shard_map/psum | solution.py:43
  659.2 2.9 cholesky.186
  663.5 2.4 custom-call.18
  669.1 2.9 cholesky.241
  673.3 2.4 custom-call.23
  678.9 24.0 %all-reduce.10 = (bf16[32,256]{1,0:T(8,128)(2,1)S(1)}, bf16[32,256]{1,0:T(8,128)(2,1)S(1)}) all-reduce(f32[32,256]{1,0:T(8,128)S(1)} %fusion.68, f32[32,256]{1,0:T(8,128)S(1)} %fusion.79), channel_id=1, replica_groups=mesh['dp'=32,'tensor'=8] {'tensor'}, use_global_device_ids=true, to_apply=%region_11.0 | all-reduce | flops 16384 | bytes 98304 | tf_op jit(solution)/shard_map/psum | solution.py:35
  705.1 3.6 fusion.92
  708.7 147.6 %all-reduce.28.cloned.1.call-done = (f32[32,6656]{1,0:T(8,128)}, f32[32,2048]{1,0:T(8,128)}) async-done(((f32[32,6656]{1,0:T(8,128)}, f32[32,2048]{1,0:T(8,128)}), (f32[32,6656]{1,0:T(8,128)}, f32[32,2048]{1,0:T(8,128)})) %all-reduce.28.cloned.1.call-update) | async-done | bytes 1114128 | tf_op jit(solution)/shard_map/psum | solution.py:42
  859.9 20.7 %all-reduce.9 = (f32[32,32]{0,1:T(8,128)S(1)}, f32[32,32]{0,1:T(8,128)S(1)}) all-reduce(f32[32,32]{0,1:T(8,128)S(1)} %fusion.69, f32[32,32]{0,1:T(8,128)S(1)} %fusion.80), channel_id=1, replica_groups=mesh['dp'=32,'tensor'=8] {'tensor'}, use_global_device_ids=true, to_apply=%region_13.0 | all-reduce | flops 2048 | bytes 16384 | tf_op jit(solution)/shard_map/psum | solution.py:43
  880.7 2.9 cholesky.197
  884.9 2.4 custom-call.19
  889.4 3.0 fusion.70
  892.5 2.9 cholesky.252
  896.8 2.4 custom-call.24
  902.3 24.0 %all-reduce.8 = (bf16[32,256]{1,0:T(8,128)(2,1)S(1)}, bf16[32,256]{1,0:T(8,128)(2,1)S(1)}) all-reduce(f32[32,256]{1,0:T(8,128)S(1)} %fusion.70, f32[32,256]{1,0:T(8,128)S(1)} %fusion.81), channel_id=1, replica_groups=mesh['dp'=32,'tensor'=8] {'tensor'}, use_global_device_ids=true, to_apply=%region_14.0 | all-reduce | flops 16384 | bytes 98304 | tf_op jit(solution)/shard_map/psum | solution.py:35
  930.3 147.4 %all-reduce.26.cloned.1.call-done = (f32[32,2048]{1,0:T(8,128)}, f32[32,6656]{1,0:T(8,128)}) async-done(((f32[32,2048]{1,0:T(8,128)}, f32[32,6656]{1,0:T(8,128)}), (f32[32,2048]{1,0:T(8,128)}, f32[32,6656]{1,0:T(8,128)})) %all-reduce.26.cloned.1.call-update) | async-done | bytes 1114128 | tf_op jit(solution)/shard_map/psum | solution.py:42
  1079.1 2.2 fusion.82
  1081.4 20.7 %all-reduce.7 = (f32[32,32]{0,1:T(8,128)S(1)}, f32[32,32]{0,1:T(8,128)S(1)}) all-reduce(f32[32,32]{0,1:T(8,128)S(1)} %fusion.71, f32[32,32]{0,1:T(8,128)S(1)} %fusion.82), channel_id=1, replica_groups=mesh['dp'=32,'tensor'=8] {'tensor'}, use_global_device_ids=true, to_apply=%region_16.0 | all-reduce | flops 2048 | bytes 16384 | tf_op jit(solution)/shard_map/psum | solution.py:43
  1102.2 2.9 cholesky.208
  1106.4 2.4 custom-call.20
  1109.0 2.9 cholesky.263
  1113.2 2.4 custom-call.25
  1119.4 2.9 convert_multiply_fusion
  1123.4 24.0 %all-reduce.6 = (bf16[32,256]{1,0:T(8,128)(2,1)S(1)}, bf16[32,256]{1,0:T(8,128)(2,1)S(1)}) all-reduce(f32[32,256]{1,0:T(8,128)S(1)} %fusion.72, f32[32,256]{1,0:T(8,128)S(1)} %fusion.83), channel_id=1, replica_groups=mesh['dp'=32,'tensor'=8] {'tensor'}, use_global_device_ids=true, to_apply=%region_17.0 | all-reduce | flops 16384 | bytes 98304 | tf_op jit(solution)/shard_map/psum | solution.py:35
  1149.6 3.6 fusion.90
  1153.1 147.7 %all-reduce.24.cloned.1.call-done = (f32[32,6656]{1,0:T(8,128)}, f32[32,2048]{1,0:T(8,128)}) async-done(((f32[32,6656]{1,0:T(8,128)}, f32[32,2048]{1,0:T(8,128)}), (f32[32,6656]{1,0:T(8,128)}, f32[32,2048]{1,0:T(8,128)})) %all-reduce.24.cloned.1.call-update) | async-done | bytes 1114128 | tf_op jit(solution)/shard_map/psum | solution.py:59
  (102 shorter events, 73.3 us)
Async XLA Ops:
  7.2 29.2 %copy-start = (bf16[256,6656]{1,0:T(8,128)(2,1)S(1)}, bf16[256,6656]{1,0:T(8,128)(2,1)}, u32[]{:S(2)}) copy-start(bf16[256,6656]{1,0:T(8,128)(2,1)} %param.13) | copy-start | bytes 10223620
  7.2 184.4 %all-reduce.34.cloned.1.call-start = ((), (), s32[]{:S(2)}) async-start(), calls=%async_computation.5 | async-start | bytes 2228224 | tf_op jit(solution)/shard_map/psum | solution.py:42
  7.2 3.3 copy-start.1
  7.2 3.3 copy-start.2
  38.0 375.2 %all-reduce.32.cloned.1.call-start = ((), (), s32[]{:S(2)}) async-start(), calls=%async_computation.4 | async-start | bytes 2228224 | tf_op jit(solution)/shard_map/psum | solution.py:42
  265.4 369.4 %all-reduce.30.cloned.1.call-start = ((), (), s32[]{:S(2)}) async-start(), calls=%async_computation.3 | async-start | bytes 2228224 | tf_op jit(solution)/shard_map/psum | solution.py:42
  487.1 369.1 %all-reduce.28.cloned.1.call-start = ((), (), s32[]{:S(2)}) async-start(), calls=%async_computation.2 | async-start | bytes 2228224 | tf_op jit(solution)/shard_map/psum | solution.py:42
  708.6 369.1 %all-reduce.26.cloned.1.call-start = ((), (), s32[]{:S(2)}) async-start(), calls=%async_computation.1 | async-start | bytes 2228224 | tf_op jit(solution)/shard_map/psum | solution.py:42
  930.1 370.8 %all-reduce.24.cloned.1.call-start = ((), (), s32[]{:S(2)}) async-start(), calls=%async_computation | async-start | bytes 2228224 | tf_op jit(solution)/shard_map/psum | solution.py:59
Sparse Core Ops, SparseCore 0:
  38.1 153.4 all-reduce.33
  265.5 147.5 all-reduce.31
  487.3 147.5 all-reduce.29
  708.8 147.4 all-reduce.27
  930.2 147.5 all-reduce.25
  1153.3 147.5 all-reduce.23
where the time goes:
time: 1310 us
  waiting for transfers between devices  892 us (68%)
  blocking collectives  247 us (19%)
  matrix products  86.6 us (7%)
  other arithmetic  70.7 us (5%)
  between operations  14.5 us (1%)
    psum x5, waiting for transfers between devices, orthonormal_pair(): full_one, full_two = lax.psum((result_one, result_two), 'dp')  744 us
    psum x1, waiting for transfers between devices, local(): up_image, down_image = lax.psum((up_image, down_image), 'dp')  148 us
    psum x6, blocking collectives, sketch_round(): first, second = lax.psum((first, second), 'tensor')  143 us
    psum x5, blocking collectives, orthonormal_pair(): lax.psum((self_gram(full_one), self_gram(full_two)), 'tensor')  104 us
    another operation x30, other arithmetic, normalize_rows(): lower = jnp.linalg.cholesky(gram)  36 us
    another operation x20, other arithmetic, normalize_rows(): jax.scipy.linalg.solve_triangular(lower, panel, lower=True)  30.9 us
  transfers between devices with their start and end apart: 6, of which 6 were waited for; matrix products, arithmetic and copies ran while one was open for 0% of the time, Pallas kernels for 0%

commit v1 on v0

v1 whole, which is shorter than its diff:
```python
import functools
import math

import jax
import jax.numpy as jnp
from jax import lax
from jax.experimental import pallas as pl
from jax.experimental.pallas import tpu as pltpu
from jax.sharding import PartitionSpec as P

MESH = pl.DeviceIdType.MESH

NZ, NY, NX, NC = 8, 4, 4, 2
R = 32
ITERS = 2
ROUNDS = 2 * ITERS + 2
HALF = R // 2
LANES = 128
GROUPS = NZ // 2
SLOTS = NZ * NY

FAR = (4, 3, 5, 2, 6, 1, 7)
NEAR = (1, 7, 2, 6, 3, 5, 4)


def nt_dot(a, b):
    return lax.dot_general(a, b, (((1,), (1,)), ((), ())), preferred_element_type=jnp.float32)


def nn_dot(a, b, precision=None):
    return lax.dot_general(
        a, b, (((1,), (0,)), ((), ())), precision=precision, preferred_element_type=jnp.float32
    )


def invert_factor(gram):
    lane = lax.broadcasted_iota(jnp.int32, (R, LANES), 1)
    row = lax.broadcasted_iota(jnp.int32, (R, LANES), 0)
    wide = lane < 64
    right = (lane % 64) >= R
    eye = jnp.where((lane % 64) - R == row, 1.0, 0.0)
    work = jnp.where(right, eye, gram)
    pivots = jnp.zeros((R, LANES), jnp.float32)
    for k in range(R):
        column = jnp.where(
            wide,
            jnp.broadcast_to(work[:, k : k + 1], (R, LANES)),
            jnp.broadcast_to(work[:, 64 + k : 65 + k], (R, LANES)),
        )
        pivot = jnp.broadcast_to(column[k : k + 1, :], (R, LANES))
        pivots = jnp.where(row == k, pivot, pivots)
        factor = jnp.where(row > k, column / pivot, 0.0)
        work = work - factor * jnp.broadcast_to(work[k : k + 1, :], (R, LANES))
    return jnp.where(right, work * lax.rsqrt(pivots), 0.0)


def kernel(
    x_in, grad_up, hidden_act, grad_down, sketch_up, sketch_down,
    up_a, up_b, down_a, down_b,
    wide, narrow, sk_wide, sk_narrow, panel, ysend, yrecv, zown, zsend, zrecv,
    us, uc, ux, kparts, kbuf,
    in_sem, ys_sem, yr_sem, zs_sem, zr_sem, ag_sem, agz_sem, agy_sem,
    ks_sem, kr_sem, ucs_sem, ucr_sem, uxs_sem, uxr_sem,
):
    dp = lax.axis_index("dp")
    me_t = lax.axis_index("tensor")
    z, y = dp // NY, dp % NY
    x, c = me_t // NC, me_t % NC
    slot = dp
    tiles_wide = wide.shape[2] // LANES // GROUPS
    tiles_narrow = narrow.shape[2] // LANES // GROUPS
    span = tiles_wide // NY
    cols_wide = tiles_wide * LANES
    cols_narrow = tiles_narrow * LANES
    tokens = wide.shape[1]

    loads = [
        pltpu.make_async_copy(src, dst, in_sem.at[i])
        for i, (src, dst) in enumerate(
            (
                (sketch_up, sk_wide),
                (sketch_down, sk_narrow),
                (grad_up, wide.at[0]),
                (grad_down, narrow.at[1]),
                (x_in, narrow.at[0]),
                (hidden_act, wide.at[1]),
            )
        )
    ]
    for load in loads:
        load.start()

    def dev_zy(zz, yy):
        return (zz * NY + yy, me_t)

    def dev_t(tt):
        return (dp, tt)

    barrier = pltpu.get_barrier_semaphore()
    peers = [dev_zy((z + o) % NZ, y) for o in range(1, NZ)]
    peers += [dev_zy(z, (y + o) % NY) for o in range(1, NY)]
    peers += [dev_t((me_t + o) % (NX * NC)) for o in range(1, NX * NC)]
    for peer in peers:
        pl.semaphore_signal(barrier, inc=1, device_id=peer, device_id_type=MESH)

    for load in loads:
        load.wait()

    for k in range(GROUPS):
        for h in range(2):
            for yy in range(NY):
                s = (2 * k + h) * NY + yy
                rows = slice(HALF * h, HALF * h + HALF)
                for i in range(span + 1):
                    lo = (k * tiles_wide + yy * span + i) * LANES
                    panel[0, s, i] = sk_wide[rows, lo : lo + LANES]
                lo = (k * tiles_narrow + yy) * LANES
                panel[0, s, span + 1] = sk_narrow[rows, lo : lo + LANES]

    pl.semaphore_wait(barrier, len(peers))

    def unpack(r, kk):
        wide_tiles, narrow_tiles = [], []
        for t in range(tiles_wide):
            yy = min(t // span, NY - 1)
            i = t - span * yy
            wide_tiles.append(
                jnp.concatenate([panel[r, (2 * kk + h) * NY + yy, i] for h in range(2)], axis=0)
            )
        for yy in range(NY):
            narrow_tiles.append(
                jnp.concatenate([panel[r, (2 * kk + h) * NY + yy, span + 1] for h in range(2)], axis=0)
            )
        return jnp.concatenate(wide_tiles, axis=1), jnp.concatenate(narrow_tiles, axis=1)

    def wait_gather(kk):
        part = panel.at[0, pl.ds(0, 2 * (NY - 1))]
        pltpu.make_async_copy(part, part, agy_sem.at[kk]).wait()

    def wait_sends():
        for buf, n, sem in (
            (ysend.at[0], NZ * (NY - 1), ys_sem),
            (zsend.at[0], NZ - 1, zs_sem),
            (panel.at[0], NZ - 1 + NZ * (NY - 1), ag_sem),
            (kbuf.at[0], NX * NC - 1, ks_sem),
            (us, 1, ucs_sem),
            (ux.at[0], (NX - 1) * NC, uxs_sem),
        ):
            part = buf.at[pl.ds(0, n)]
            pltpu.make_async_copy(part, part, sem).wait()

    def one_round(r, _):
        par = r % 2
        sum_wide = jnp.zeros((R, tokens), jnp.float32)
        sum_narrow = jnp.zeros((R, tokens), jnp.float32)
        for o in (0, 1, 3, 2):
            kk = (z // 2 + o) % GROUPS

            @pl.when(r > 0)
            def _():
                wait_gather(kk)

            pw, pn = unpack(r, kk)
            at_wide = pl.ds(pl.multiple_of(kk * cols_wide, LANES), cols_wide)
            at_narrow = pl.ds(pl.multiple_of(kk * cols_narrow, LANES), cols_narrow)
            kparts[kk, 0] = nt_dot(pw, pw)
            kparts[kk, 1] = nt_dot(pn, pn)
            sum_wide = sum_wide + nt_dot(pw, wide[par, :, at_wide])
            sum_narrow = sum_narrow + nt_dot(pn, narrow[1 - par, :, at_narrow])

        kw = ((kparts[0, 0] + kparts[1, 0]) + kparts[2, 0]) + kparts[3, 0]
        kn = ((kparts[0, 1] + kparts[1, 1]) + kparts[2, 1]) + kparts[3, 1]
        blank = jnp.zeros((R, R), jnp.float32)
        kbuf[r, me_t] = jnp.concatenate([kw, blank, kn, blank], axis=1)
        us[r, 0] = sum_wide
        us[r, 1] = sum_narrow
        pltpu.make_async_remote_copy(
            us.at[r], uc.at[r], ucs_sem, ucr_sem.at[r],
            device_id=dev_t(x * NC + 1 - c), device_id_type=MESH,
        ).start()
        for o in range(1, NX * NC):
            pltpu.make_async_remote_copy(
                kbuf.at[r, me_t], kbuf.at[r, me_t], ks_sem, kr_sem.at[r],
                device_id=dev_t((me_t + o) % (NX * NC)), device_id_type=MESH,
            ).start()

        pltpu.make_async_copy(us.at[r], uc.at[r], ucr_sem.at[r]).wait()
        ux[r, x * NC] = (us[r, 0] + uc[r, 0]).astype(jnp.bfloat16)
        ux[r, x * NC + 1] = (us[r, 1] + uc[r, 1]).astype(jnp.bfloat16)
        for o in range(1, NX):
            for cc in range(NC):
                pltpu.make_async_remote_copy(
                    ux.at[r, me_t], ux.at[r, me_t], uxs_sem, uxr_sem.at[r],
                    device_id=dev_t(((x + o) % NX) * NC + cc), device_id_type=MESH,
                ).start()

        part = kbuf.at[r, pl.ds(0, NX * NC - 1)]
        pltpu.make_async_copy(part, part, kr_sem.at[r]).wait()
        gram = kbuf[r, 0]
        for t in range(1, NX * NC):
            gram = gram + kbuf[r, t]
        lane = lax.broadcasted_iota(jnp.int32, (R, LANES), 1)
        row = lax.broadcasted_iota(jnp.int32, (R, LANES), 0)
        identity = jnp.where((lane % 64) - R == row, 1.0, 0.0)
        inverse = jnp.where(jnp.full((R, LANES), r) == 0, identity, invert_factor(gram))
        inv_wide = inverse[:, R : 2 * R]
        inv_narrow = inverse[:, 64 + R : 64 + 2 * R]

        part = ux.at[r, pl.ds(0, (NX - 1) * NC)]
        pltpu.make_async_copy(part, part, uxr_sem.at[r]).wait()
        tok = []
        for h, inv in enumerate((inv_wide, inv_narrow)):
            total = ux[r, h].astype(jnp.float32)
            for xx in range(1, NX):
                total = total + ux[r, xx * NC + h].astype(jnp.float32)
            tok.append(nn_dot(inv, total, lax.Precision.HIGHEST).astype(jnp.bfloat16))
        tok_wide, tok_narrow = tok

        for o in (2, 1, 3, 0):
            kk = (z // 2 + o) % GROUPS
            at_wide = pl.ds(pl.multiple_of(kk * cols_wide, LANES), cols_wide)
            at_narrow = pl.ds(pl.multiple_of(kk * cols_narrow, LANES), cols_narrow)
            pw = nn_dot(tok_narrow, wide[1 - par, :, at_wide]).astype(jnp.bfloat16)
            pn = nn_dot(tok_wide, narrow[par, :, at_narrow]).astype(jnp.bfloat16)
            for h in range(2):
                rows = slice(HALF * h, HALF * h + HALF)
                for yy in range(NY):
                    s = (2 * kk + h) * NY + yy
                    for i in range(span + 1):
                        lo = (yy * span + i) * LANES
                        ysend[r, s, i] = pw[rows, lo : lo + LANES]
                    ysend[r, s, span + 1] = pn[rows, yy * LANES : (yy + 1) * LANES]
            for h in range(2):
                zd = 2 * kk + h
                for q in range(1, NY):
                    yd = (y + q) % NY
                    pltpu.make_async_remote_copy(
                        ysend.at[r, zd * NY + yd], yrecv.at[r, zd, q - 1], ys_sem, yr_sem.at[zd],
                        device_id=dev_zy(z, yd), device_id_type=MESH,
                    ).start()

        @pl.when(r == ROUNDS - 1)
        def _():
            total_wide = wide.shape[2] * NX * NC
            total_narrow = narrow.shape[2] * NX * NC
            for k in range(GROUPS):
                pw, pn = unpack(r, k)
                for inv, pan, out, cols, total in (
                    (inv_wide, pw, down_a, cols_wide, total_wide),
                    (inv_narrow, pn, up_a, cols_narrow, total_narrow),
                ):
                    q = nn_dot(inv, pan.astype(jnp.float32), lax.Precision.HIGHEST)
                    q = q.astype(jnp.bfloat16).astype(jnp.float32) * math.sqrt(total)
                    out[:, k * cols : (k + 1) * cols] = q

        for o in FAR + (0,):
            zd = (z + o) % NZ
            part = yrecv.at[r, zd]
            pltpu.make_async_copy(part, part, yr_sem.at[zd]).wait()
            total = ysend[r, zd * NY + y].astype(jnp.float32)
            for q in range(NY - 1):
                total = total + yrecv[r, zd, q].astype(jnp.float32)
            if o:
                zsend[r, zd] = total.astype(jnp.bfloat16)
                pltpu.make_async_remote_copy(
                    zsend.at[r, zd], zrecv.at[r, o - 1], zs_sem, zr_sem,
                    device_id=dev_zy(zd, y), device_id_type=MESH,
                ).start()
            else:
                zown[...] = total
        part = zrecv.at[r]
        pltpu.make_async_copy(part, part, zr_sem).wait()
        total = zown[...]
        for q in range(NZ - 1):
            total = total + zrecv[r, q].astype(jnp.float32)
        panel[r + 1, slot] = total.astype(jnp.bfloat16)

        def to_y(zs):
            s = zs * NY + y
            for q in range(1, NY):
                pltpu.make_async_remote_copy(
                    panel.at[r + 1, s], panel.at[r + 1, s], ag_sem, agy_sem.at[zs // 2],
                    device_id=dev_zy(z, (y + q) % NY), device_id_type=MESH,
                ).start()

        for o in FAR:
            pltpu.make_async_remote_copy(
                panel.at[r + 1, slot], panel.at[r + 1, slot], ag_sem, agz_sem.at[o - 1],
                device_id=dev_zy((z + o) % NZ, y), device_id_type=MESH,
            ).start()
        to_y(z)
        for o in NEAR:
            zs = (z + NZ - o) % NZ
            part = panel.at[r + 1, zs * NY + y]
            pltpu.make_async_copy(part, part, agz_sem.at[o - 1]).wait()
            to_y(zs)
        wait_sends()
        return 0

    lax.fori_loop(0, ROUNDS, one_round, 0)

    scale = 1.0 / math.sqrt(tokens * NZ * NY)
    for k in range(GROUPS):
        wait_gather(k)
    for k in range(GROUPS):
        pw, pn = unpack(ROUNDS, k)
        up_b[:, k * cols_wide : (k + 1) * cols_wide] = pw.astype(jnp.float32) * scale
        down_b[:, k * cols_narrow : (k + 1) * cols_narrow] = pn.astype(jnp.float32) * scale


def local(x_in, grad_up, hidden_act, grad_down, sketch_up, sketch_down):
    tokens, n_narrow = x_in.shape
    n_wide = grad_up.shape[1]
    piece = (n_wide // LANES // GROUPS // NY + 2, HALF, LANES)
    bf16, f32 = jnp.bfloat16, jnp.float32
    dma = pltpu.SemaphoreType.DMA
    vmem = pltpu.VMEM
    scratch = [
        vmem((2, tokens, n_wide), bf16),
        vmem((2, tokens, n_narrow), bf16),
        vmem((R, n_wide), bf16),
        vmem((R, n_narrow), bf16),
        vmem((ROUNDS + 1, SLOTS) + piece, bf16),
        vmem((ROUNDS, SLOTS) + piece, bf16),
        vmem((ROUNDS, NZ, NY - 1) + piece, bf16),
        vmem(piece, f32),
        vmem((ROUNDS, NZ) + piece, bf16),
        vmem((ROUNDS, NZ - 1) + piece, bf16),
        vmem((ROUNDS, 2, R, tokens), f32),
        vmem((ROUNDS, 2, R, tokens), f32),
        vmem((ROUNDS, NX * NC, R, tokens), bf16),
        vmem((GROUPS, 2, R, R), f32),
        vmem((ROUNDS, NX * NC, R, LANES), f32),
        dma((6,)), dma, dma((NZ,)), dma, dma, dma, dma((NZ - 1,)), dma((GROUPS,)),
        dma, dma((ROUNDS,)), dma, dma((ROUNDS,)), dma, dma((ROUNDS,)),
    ]
    out_shape = (
        jax.ShapeDtypeStruct((R, n_narrow), f32),
        jax.ShapeDtypeStruct((R, n_wide), f32),
        jax.ShapeDtypeStruct((R, n_wide), f32),
        jax.ShapeDtypeStruct((R, n_narrow), f32),
    )
    return pl.pallas_call(
        kernel,
        out_shape=out_shape,
        in_specs=[pl.BlockSpec(memory_space=pl.ANY)] * 6,
        out_specs=[pl.BlockSpec(memory_space=pltpu.VMEM)] * 4,
        scratch_shapes=scratch,
        compiler_params=pltpu.CompilerParams(
            collective_id=0, has_side_effects=True, vmem_limit_bytes=56 * 2**20
        ),
    )(x_in, grad_up, hidden_act, grad_down, sketch_up, sketch_down)


def solution(mesh):
    in_specs = (
        P("dp", "tensor"),
        P("dp", "tensor"),
        P("dp", "tensor"),
        P("dp", "tensor"),
        P(None, "tensor"),
        P(None, "tensor"),
    )
    out_specs = (P(None, "tensor"), P(None, "tensor"), P(None, "tensor"), P(None, "tensor"))
    return jax.shard_map(local, mesh=mesh, in_specs=in_specs, out_specs=out_specs, check_vma=False)
```

time: 1310 us -> 225 us (0.17)
  waiting for transfers between devices: 892 us -> 0 us
  blocking collectives: 247 us -> 0 us
  Pallas kernels: 0 us -> 215 us
  matrix products: 86.6 us -> 0 us
  other arithmetic: 70.7 us -> 0 us
  between operations: 14.5 us -> 0.65 us
    psum x6 -> x0, waiting for transfers between devices: 892 us -> none  [the longest x5 744 us: orthonormal_pair(): full_one, full_two = lax.psum((result_one, result_two), 'dp')]
    psum x11 -> x0, blocking collectives: 247 us -> none  [the longest x6 143 us: sketch_round(): first, second = lax.psum((first, second), 'tensor')]
    pallas_call x0 -> x1, Pallas kernels: none -> 215 us  [local(): pl.pallas_call(kernel, out_shape=out_shape, in_specs=[pl.BlockSpec(memory...]
    dot_general x34 -> x0, matrix products: 67.8 us -> none  [the longest x12 21 us: contract(): lax.dot_general(panel, rows, (((1,), (1,)), ((), ())), preferred_element_...]
    another operation x50 -> x0, other arithmetic: 66.9 us -> none  [the longest x30 36 us: normalize_rows(): lower = jnp.linalg.cholesky(gram)]
    another operation x10 -> x0, matrix products: 18.8 us -> none  [normalize_rows(): jax.scipy.linalg.solve_triangular(lower, panel, lower=True)]
  transfers between devices with their start and end apart: 6 -> 0, of which waited for: 6 -> 0; matrix products, arithmetic and copies ran while one was open for 0% -> 0% of each run, Pallas kernels for 0% -> 0%
where the time goes in v1:
time: 225 us; the launch traced here: 223 us
  Pallas kernels  215 us (96%)
  local copies, waits for them, and re-layouts  6.64 us (3%)
    pallas_call x1, Pallas kernels, local(): pl.pallas_call(kernel, out_shape=out_shape, in_specs=[pl.BlockSpec(memory...  215 us
    unnamed x6, local copies, waits for them, and re-layouts  6.64 us

profile of v1, /device:TPU:2, one launch (start us, length us, event | category | flops | bytes accessed | tf_op | source)
XLA Modules:
  0.0 222.8 jit_solution(295307238772637660)
XLA Ops:
  0.6 215.5 %shard_map.93 = (f32[32,2048]{1,0:T(8,128)}, f32[32,6656]{1,0:T(8,128)}, f32[32,6656]{1,0:T(8,128)}, f32[32,2048]{1,0:T(8,128)}) custom-call(bf16[256,2048]{1,0:T(8,128)(2,1)} %x_in.1, bf16[256,6656]{1,0:T(8,128)(2,1)} %grad_up.1, bf16[256,6656]{1,0:T(8,128)(2,1)} %hidden_act.1, bf16[256,2048]{1,0:T(8,128)(2,1)} %grad_down.1, bf16[32,6656]{1,0:T(8,128)(2,1)} %sketch_up.1, ...), custom_call_target="tpu_custom_call" | custom-call | tf_op jit(solution)/shard_map/pallas_call | solution.py:343
  216.1 0.0 copy-start
  216.1 1.7 copy.14
  217.9 2.1 copy.15
  220.0 2.1 copy.16
  222.1 0.0 copy-done
  222.1 0.7 copy.17
Async XLA Ops:
  216.1 5.9 %copy-start = (f32[32,2048]{1,0:T(8,128)S(1)}, f32[32,2048]{1,0:T(8,128)}, u32[]{:S(2)}) copy-start(f32[32,2048]{1,0:T(8,128)} %get-tuple-element.11) | copy-start | bytes 786436

commit v2 on v0

v2 whole, which is shorter than its diff:
```python
import functools
import math

import jax
import jax.numpy as jnp
from jax import lax
from jax.experimental import pallas as pl
from jax.experimental.pallas import tpu as pltpu
from jax.sharding import PartitionSpec as P

MESH = pl.DeviceIdType.MESH

NZ, NY, NX, NC = 8, 4, 4, 2
R = 32
ITERS = 2
PAIRS = ITERS + 1
HALF = R // 2
LANES = 128
GROUPS = NZ // 2
SLOTS = NZ * NY
NT = NX * NC
BLOCK = 16

FAR = (4, 3, 5, 2, 6, 1, 7)
NEAR = (1, 7, 2, 6, 3, 5, 4)


def nt_dot(a, b):
    return lax.dot_general(a, b, (((1,), (1,)), ((), ())), preferred_element_type=jnp.float32)


def nn_dot(a, b, precision=None):
    return lax.dot_general(
        a, b, (((1,), (0,)), ((), ())), precision=precision, preferred_element_type=jnp.float32
    )


def invert_factor(gram):
    lane = lax.broadcasted_iota(jnp.int32, (R, LANES), 1)
    row = lax.broadcasted_iota(jnp.int32, (R, LANES), 0)
    right = lane >= R
    padded = jnp.concatenate([gram, jnp.zeros((R, LANES - R), jnp.float32)], axis=1)
    work = jnp.where(right, jnp.where(lane - R == row, 1.0, 0.0), padded)
    scale = jnp.zeros((R, LANES), jnp.float32)
    for b in range(0, R, BLOCK):
        cols = [jnp.broadcast_to(work[:, b + j : b + j + 1], (R, LANES)) for j in range(BLOCK)]
        for j in range(BLOCK):
            k = b + j
            pivot = jnp.broadcast_to(cols[j][k : k + 1, :], (R, LANES))
            scale = jnp.where(row == k, lax.rsqrt(pivot), scale)
            factor = jnp.where(row > k, cols[j] * (1.0 / pivot), 0.0)
            for i in range(j + 1, BLOCK):
                cols[i] = cols[i] - factor * jnp.broadcast_to(cols[i][k : k + 1, :], (R, LANES))
            work = work - factor * jnp.broadcast_to(work[k : k + 1, :], (R, LANES))
    return (work * scale)[:, R : 2 * R]


def settle(ref, sem):
    pltpu.make_async_copy(ref, ref, sem).wait()


def kernel(
    x_in, grad_up, hidden_act, grad_down, sketch_up, sketch_down,
    up_q, up_img, down_q, down_img,
    x_v, gu_v, h_v, gd_v, sk_wide, sk_narrow, qn_v, qw_v,
    up_wide, up_narrow, dn_wide, dn_narrow,
    ysend, yrecv, zown, zsend, zrecv, nsend, nrecv,
    us, uc, ux, kparts, kbuf,
    in_sem, out_sem, ys_sem, yr_sem, zs_sem, zr_sem, ag_sem, agz_sem, agy_sem,
    ns_sem, nr_sem, nag_sem, nagr_sem, ks_sem, kr_sem, ucs_sem, ucr_sem, uxs_sem, uxr_sem,
):
    dp = lax.axis_index("dp")
    me_t = lax.axis_index("tensor")
    z, y = dp // NY, dp % NY
    x, c = me_t // NC, me_t % NC
    slot = dp
    n_wide, n_narrow = gu_v.shape[1], x_v.shape[1]
    tiles = n_wide // LANES // GROUPS
    span = tiles // NY
    cols = tiles * LANES
    tokens = gu_v.shape[0]

    loads = [
        pltpu.make_async_copy(src, dst, in_sem.at[i])
        for i, (src, dst) in enumerate(
            (
                (sketch_down, sk_narrow),
                (sketch_up, sk_wide),
                (grad_down, gd_v),
                (grad_up, gu_v),
                (hidden_act, h_v),
                (x_in, x_v),
            )
        )
    ]
    for load in loads:
        load.start()

    def dev_dp(zz, yy):
        return (zz * NY + yy, me_t)

    def dev_t(tt):
        return (dp, tt)

    def send(src, dst, send_sem, recv_sem, device):
        pltpu.make_async_remote_copy(
            src, dst, send_sem, recv_sem, device_id=device, device_id_type=MESH
        ).start()

    barrier = pltpu.get_barrier_semaphore()
    peers = [((dp + o) % SLOTS, me_t) for o in range(1, SLOTS)]
    peers += [dev_t((me_t + o) % NT) for o in range(1, NT)]
    for peer in peers:
        pl.semaphore_signal(barrier, inc=1, device_id=peer, device_id_type=MESH)

    for load in loads[:4]:
        load.wait()

    for k in range(GROUPS):
        for h in range(2):
            rows = slice(HALF * h, HALF * h + HALF)
            for yy in range(NY):
                s = (2 * k + h) * NY + yy
                for i in range(span + 1):
                    lo = (k * tiles + yy * span + i) * LANES
                    up_wide[0, s, i] = sk_wide[rows, lo : lo + LANES]
                lo = (k * NY + yy) * LANES
                dn_narrow[0, s] = sk_narrow[rows, lo : lo + LANES]

    pl.semaphore_wait(barrier, len(peers))

    def wide_group(panel, i, kk):
        out = []
        for t in range(tiles):
            yy = min(t // span, NY - 1)
            out.append(
                jnp.concatenate(
                    [panel[i, (2 * kk + h) * NY + yy, t - span * yy] for h in range(2)], axis=0
                )
            )
        return jnp.concatenate(out, axis=1)

    def narrow_all(panel, i):
        out = []
        for t in range(SLOTS // 2):
            k, yy = t // NY, t % NY
            out.append(
                jnp.concatenate([panel[i, (2 * k + h) * NY + yy] for h in range(2)], axis=0)
            )
        return jnp.concatenate(out, axis=1)

    def send_gram(cp, d, gram):
        packed = jnp.concatenate([gram[8 * j : 8 * j + 8, :] for j in range(R // 8)], axis=1)
        kbuf[cp, d, me_t] = packed
        mine = kbuf.at[cp, d, me_t]
        for o in (1, 2, 3, 4, 5, 6, 7):
            send(mine, mine, ks_sem.at[cp], kr_sem.at[cp, d], dev_t((me_t + o) % NT))

    def send_core(cp, d, total):
        us[cp, d] = total
        send(us.at[cp, d], uc.at[cp, d], ucs_sem.at[cp], ucr_sem.at[cp, d], dev_t(x * NC + 1 - c))

    def past_sends(cp, d):
        @pl.when(d > 0)
        def _():
            last_tensor(cp)

    def last_tensor(cp):
        settle(kbuf.at[cp, 0, pl.ds(0, NT - 1)], ks_sem.at[cp])
        settle(us.at[cp, 0], ucs_sem.at[cp])
        settle(ux.at[cp, 0, pl.ds(0, (NX - 1) * NC)], uxs_sem.at[cp])

    def last_wide(w):
        settle(ysend.at[w, 0, pl.ds(0, NZ * (NY - 1))], ys_sem.at[w])
        settle(zsend.at[w, 0, pl.ds(0, NZ - 1)], zs_sem.at[w])
        settle(up_wide.at[0, pl.ds(0, SLOTS - 1)], ag_sem.at[w])

    def last_narrow(w):
        settle(nsend.at[w, 0, pl.ds(0, SLOTS - 1)], ns_sem.at[w])
        settle(up_narrow.at[0, pl.ds(0, SLOTS - 1)], nag_sem.at[w])

    def wait_wide(w, kk):
        settle(up_wide.at[0, pl.ds(0, 2 * (NY - 1))], agy_sem.at[w, kk])

    def wait_narrow(w):
        settle(up_narrow.at[0, pl.ds(0, SLOTS - 1)], nagr_sem.at[w])

    def sums_wide(cp, d, panel, w, rows, fresh):
        past_sends(cp, d)
        total = jnp.zeros((R, tokens), jnp.float32)
        for n, o in enumerate((0, 1, 3, 2)):
            kk = (z // 2 + o) % GROUPS
            if fresh:
                wait_wide(w, kk)
            else:

                @pl.when(d > 0)
                def _():
                    wait_wide(w, kk)

            part = wide_group(panel, d, kk)
            kparts[kk] = nt_dot(part, part)
            if n == GROUPS - 1:
                send_gram(cp, d, ((kparts[0] + kparts[1]) + kparts[2]) + kparts[3])
            at = pl.ds(pl.multiple_of(kk * cols, LANES), cols)
            total = total + nt_dot(part, rows[:, at])
        send_core(cp, d, total)

    def sums_narrow(cp, d, panel, w, rows, fresh):
        past_sends(cp, d)
        if fresh:
            wait_narrow(w)
        else:

            @pl.when(d > 0)
            def _():
                wait_narrow(w)

        part = narrow_all(panel, d)
        send_gram(cp, d, nt_dot(part, part))
        send_core(cp, d, nt_dot(part, rows[...]))

    def over_chip(cp, d):
        settle(uc.at[cp, d], ucr_sem.at[cp, d])
        total = (us[cp, d] + uc[cp, d]).astype(jnp.bfloat16)
        for h in range(2):
            ux[cp, d, x * NC + h] = total[HALF * h : HALF * h + HALF]
        mine = ux.at[cp, d, me_t]
        for o in (2, 1, 3):
            for cc in range(NC):
                send(mine, mine, uxs_sem.at[cp], uxr_sem.at[cp, d], dev_t(((x + o) % NX) * NC + cc))

    def tokens_done(cp, d, first):
        settle(kbuf.at[cp, d, pl.ds(0, NT - 1)], kr_sem.at[cp, d])
        packed = kbuf[cp, d, 0]
        for t in range(1, NT):
            packed = packed + kbuf[cp, d, t]
        gram = jnp.concatenate([packed[:, R * j : R * j + R] for j in range(R // 8)], axis=0)
        inverse = invert_factor(gram)
        if first:
            row = lax.broadcasted_iota(jnp.int32, (R, R), 0)
            col = lax.broadcasted_iota(jnp.int32, (R, R), 1)
            identity = jnp.where(row == col, 1.0, 0.0)
            inverse = jnp.where(jnp.full((R, R), d) == 0, identity, inverse)
        settle(ux.at[cp, d, pl.ds(0, (NX - 1) * NC)], uxr_sem.at[cp, d])
        halves = []
        for h in range(2):
            total = ux[cp, d, h].astype(jnp.float32)
            for xx in range(1, NX):
                total = total + ux[cp, d, xx * NC + h].astype(jnp.float32)
            halves.append(total)
        total = jnp.concatenate(halves, axis=0)
        return inverse, nn_dot(inverse, total, lax.Precision.HIGHEST).astype(jnp.bfloat16)

    def scatter_wide(w, d, tok, rows):
        @pl.when(d > 0)
        def _():
            last_wide(w)

        for o in (2, 1, 3, 0):
            kk = (z // 2 + o) % GROUPS
            at = pl.ds(pl.multiple_of(kk * cols, LANES), cols)
            part = nn_dot(tok, rows[:, at]).astype(jnp.bfloat16)
            for h in range(2):
                for yy in range(NY):
                    for i in range(span + 1):
                        lo = (yy * span + i) * LANES
                        ysend[w, d, (2 * kk + h) * NY + yy, i] = part[
                            HALF * h : HALF * h + HALF, lo : lo + LANES
                        ]
            for h in range(2):
                zd = 2 * kk + h
                for q in (2, 1, 3):
                    yd = (y + q) % NY
                    send(
                        ysend.at[w, d, zd * NY + yd], yrecv.at[w, d, zd, q - 1],
                        ys_sem.at[w], yr_sem.at[w, zd], dev_dp(z, yd),
                    )

    def reduce_wide(w, d):
        for o in FAR + (0,):
            zd = (z + o) % NZ
            settle(yrecv.at[w, d, zd], yr_sem.at[w, zd])
            total = ysend[w, d, zd * NY + y].astype(jnp.float32)
            for q in range(NY - 1):
                total = total + yrecv[w, d, zd, q].astype(jnp.float32)
            if o:
                zsend[w, d, zd] = total.astype(jnp.bfloat16)
                send(
                    zsend.at[w, d, zd], zrecv.at[w, d, o - 1],
                    zs_sem.at[w], zr_sem.at[w], dev_dp(zd, y),
                )
            else:
                zown[w] = total

    def to_y(w, panel, i, zs):
        piece = panel.at[i, zs * NY + y]
        for q in (2, 1, 3):
            send(piece, piece, ag_sem.at[w], agy_sem.at[w, zs // 2], dev_dp(z, (y + q) % NY))

    def gather_wide(w, d, panel, i):
        settle(zrecv.at[w, d], zr_sem.at[w])
        total = zown[w]
        for q in range(NZ - 1):
            total = total + zrecv[w, d, q].astype(jnp.float32)
        panel[i, slot] = total.astype(jnp.bfloat16)
        piece = panel.at[i, slot]
        for o in NEAR:
            send(piece, piece, ag_sem.at[w], agz_sem.at[w, o - 1], dev_dp((z + o) % NZ, y))
        to_y(w, panel, i, z)

    def forward_wide(w, panel, i, offsets):
        for o in offsets:
            zs = (z + NZ - o) % NZ
            settle(panel.at[i, zs * NY + y], agz_sem.at[w, o - 1])
            to_y(w, panel, i, zs)

    def direct(src, dst, send_sem, recv_sem):
        for o in FAR + (0,):
            for q in (2, 1, 3, 0):
                if o or q:
                    zd, yd = (z + o) % NZ, (y + q) % NY
                    send(src(zd * NY + yd), dst, send_sem, recv_sem, dev_dp(zd, yd))

    def scatter_narrow(w, d, tok, rows):
        @pl.when(d > 0)
        def _():
            last_narrow(w)

        part = nn_dot(tok, rows[...]).astype(jnp.bfloat16)
        for t in range(SLOTS // 2):
            k, yy = t // NY, t % NY
            for h in range(2):
                nsend[w, d, (2 * k + h) * NY + yy] = part[
                    HALF * h : HALF * h + HALF, t * LANES : (t + 1) * LANES
                ]
        direct(lambda s: nsend.at[w, d, s], nrecv.at[w, d, slot], ns_sem.at[w], nr_sem.at[w])

    def gather_narrow(w, d, panel, i):
        settle(nrecv.at[w, d, pl.ds(0, SLOTS - 1)], nr_sem.at[w])
        nrecv[w, d, slot] = nsend[w, d, slot]
        total = nrecv[w, d, 0].astype(jnp.float32)
        for s in range(1, SLOTS):
            total = total + nrecv[w, d, s].astype(jnp.float32)
        panel[i, slot] = total.astype(jnp.bfloat16)
        piece = panel.at[i, slot]
        direct(lambda s: piece, piece, nag_sem.at[w], nagr_sem.at[w])

    def orthonormal(inverse, part):
        return nn_dot(inverse, part.astype(jnp.float32), lax.Precision.HIGHEST).astype(jnp.bfloat16)

    def pair(d, _):
        sums_narrow(2, d, dn_narrow, 1, gd_v, False)
        sums_wide(0, d, up_wide, 0, gu_v, False)
        over_chip(2, d)
        over_chip(0, d)

        @pl.when(d == 0)
        def _():
            loads[4].wait()
            loads[5].wait()

        _, tok = tokens_done(2, d, True)
        scatter_wide(1, d, tok, h_v)
        _, tok = tokens_done(0, d, True)
        scatter_narrow(0, d, tok, x_v)
        reduce_wide(1, d)
        gather_narrow(0, d, up_narrow, d)
        gather_wide(1, d, dn_wide, d)
        sums_narrow(1, d, up_narrow, 0, x_v, True)
        forward_wide(1, dn_wide, d, NEAR[:4])
        over_chip(1, d)
        forward_wide(1, dn_wide, d, NEAR[4:])
        inverse, tok = tokens_done(1, d, False)
        scatter_wide(0, d, tok, gu_v)

        @pl.when(d == PAIRS - 1)
        def _():
            qn_v[...] = orthonormal(inverse, narrow_all(up_narrow, d))
            pltpu.make_async_copy(qn_v, up_q, out_sem.at[0]).start()

        sums_wide(3, d, dn_wide, 1, h_v, True)
        over_chip(3, d)
        reduce_wide(0, d)
        inverse, tok = tokens_done(3, d, False)
        scatter_narrow(1, d, tok, gd_v)

        @pl.when(d == PAIRS - 1)
        def _():
            for k in range(GROUPS):
                qw_v[:, k * cols : (k + 1) * cols] = orthonormal(inverse, wide_group(dn_wide, d, k))
            pltpu.make_async_copy(qw_v, down_q, out_sem.at[1]).start()

        gather_wide(0, d, up_wide, d + 1)
        forward_wide(0, up_wide, d + 1, NEAR[:4])
        gather_narrow(1, d, dn_narrow, d + 1)
        forward_wide(0, up_wide, d + 1, NEAR[4:])
        return 0

    lax.fori_loop(0, PAIRS, pair, 0)

    wait_narrow(1)
    down_out = pltpu.make_async_copy(dn_narrow.at[PAIRS], down_img, out_sem.at[2])
    down_out.start()
    for k in range(GROUPS):
        wait_wide(0, k)
    up_out = pltpu.make_async_copy(up_wide.at[PAIRS], up_img, out_sem.at[3])
    up_out.start()
    for cp in range(4):
        last_tensor(cp)
    for w in range(2):
        last_wide(w)
        last_narrow(w)
    pltpu.make_async_copy(qn_v, up_q, out_sem.at[0]).wait()
    pltpu.make_async_copy(qw_v, down_q, out_sem.at[1]).wait()
    down_out.wait()
    up_out.wait()


def finish(scales, up_q, up_img, down_q, down_img, up_a, up_b, down_a, down_b):
    up_scale, down_scale, scale = scales
    up_a[...] = up_q[...].astype(jnp.float32) * up_scale
    down_a[...] = down_q[...].astype(jnp.float32) * down_scale
    tiles = up_b.shape[1] // LANES // GROUPS
    span = tiles // NY
    for k in range(GROUPS):
        for h in range(2):
            rows = slice(HALF * h, HALF * h + HALF)
            for t in range(tiles):
                yy = min(t // span, NY - 1)
                lo = (k * tiles + t) * LANES
                piece = up_img[(2 * k + h) * NY + yy, t - span * yy]
                up_b[rows, lo : lo + LANES] = piece.astype(jnp.float32) * scale
            for yy in range(NY):
                lo = (k * NY + yy) * LANES
                piece = down_img[(2 * k + h) * NY + yy]
                down_b[rows, lo : lo + LANES] = piece.astype(jnp.float32) * scale


def local(x_in, grad_up, hidden_act, grad_down, sketch_up, sketch_down):
    tokens, n_narrow = x_in.shape
    n_wide = grad_up.shape[1]
    tail = (HALF, LANES)
    piece = (n_wide // LANES // GROUPS // NY + 1,) + tail
    bf16, f32 = jnp.bfloat16, jnp.float32
    dma = pltpu.SemaphoreType.DMA
    vmem = pltpu.VMEM
    scratch = [
        vmem((tokens, n_narrow), bf16),
        vmem((tokens, n_wide), bf16),
        vmem((tokens, n_wide), bf16),
        vmem((tokens, n_narrow), bf16),
        vmem((R, n_wide), bf16),
        vmem((R, n_narrow), bf16),
        vmem((R, n_narrow), bf16),
        vmem((R, n_wide), bf16),
        vmem((PAIRS + 1, SLOTS) + piece, bf16),
        vmem((PAIRS, SLOTS) + tail, bf16),
        vmem((PAIRS, SLOTS) + piece, bf16),
        vmem((PAIRS + 1, SLOTS) + tail, bf16),
        vmem((2, PAIRS, SLOTS) + piece, bf16),
        vmem((2, PAIRS, NZ, NY - 1) + piece, bf16),
        vmem((2,) + piece, f32),
        vmem((2, PAIRS, NZ) + piece, bf16),
        vmem((2, PAIRS, NZ - 1) + piece, bf16),
        vmem((2, PAIRS, SLOTS) + tail, bf16),
        vmem((2, PAIRS, SLOTS) + tail, bf16),
        vmem((4, PAIRS, R, tokens), f32),
        vmem((4, PAIRS, R, tokens), f32),
        vmem((4, PAIRS, NT, HALF, tokens), bf16),
        vmem((GROUPS, R, R), f32),
        vmem((4, PAIRS, NT, 8, LANES), f32),
        dma((6,)), dma((4,)), dma((2,)), dma((2, NZ)), dma((2,)), dma((2,)),
        dma((2,)), dma((2, NZ - 1)), dma((2, GROUPS)),
        dma((2,)), dma((2,)), dma((2,)), dma((2,)),
        dma((4,)), dma((4, PAIRS)), dma((4,)), dma((4, PAIRS)), dma((4,)), dma((4, PAIRS)),
    ]
    panels = pl.pallas_call(
        kernel,
        out_shape=(
            jax.ShapeDtypeStruct((R, n_narrow), bf16),
            jax.ShapeDtypeStruct((SLOTS,) + piece, bf16),
            jax.ShapeDtypeStruct((R, n_wide), bf16),
            jax.ShapeDtypeStruct((SLOTS,) + tail, bf16),
        ),
        in_specs=[pl.BlockSpec(memory_space=pl.ANY)] * 6,
        out_specs=[pl.BlockSpec(memory_space=pl.ANY)] * 4,
        scratch_shapes=scratch,
        compiler_params=pltpu.CompilerParams(
            collective_id=0, has_side_effects=True, vmem_limit_bytes=56 * 2**20
        ),
    )(x_in, grad_up, hidden_act, grad_down, sketch_up, sketch_down)
    width = lax.axis_size("tensor")
    scales = (
        math.sqrt(n_narrow * width),
        math.sqrt(n_wide * width),
        1.0 / math.sqrt(tokens * lax.axis_size("dp")),
    )
    return pl.pallas_call(
        functools.partial(finish, scales),
        out_shape=(
            jax.ShapeDtypeStruct((R, n_narrow), f32),
            jax.ShapeDtypeStruct((R, n_wide), f32),
            jax.ShapeDtypeStruct((R, n_wide), f32),
            jax.ShapeDtypeStruct((R, n_narrow), f32),
        ),
        in_specs=[pl.BlockSpec(memory_space=pltpu.VMEM)] * 4,
        out_specs=[pl.BlockSpec(memory_space=pltpu.VMEM)] * 4,
        compiler_params=pltpu.CompilerParams(vmem_limit_bytes=16 * 2**20),
    )(*panels)


def solution(mesh):
    in_specs = (
        P("dp", "tensor"),
        P("dp", "tensor"),
        P("dp", "tensor"),
        P("dp", "tensor"),
        P(None, "tensor"),
        P(None, "tensor"),
    )
    out_specs = (P(None, "tensor"), P(None, "tensor"), P(None, "tensor"), P(None, "tensor"))
    return jax.shard_map(local, mesh=mesh, in_specs=in_specs, out_specs=out_specs, check_vma=False)
```

time: 1310 us -> 176 us (0.13)
  waiting for transfers between devices: 892 us -> 0 us
  blocking collectives: 247 us -> 0 us
  Pallas kernels: 0 us -> 171 us
  matrix products: 86.6 us -> 0 us
  other arithmetic: 70.7 us -> 0 us
  between operations: 14.5 us -> 0.65 us
    psum x6 -> x0, waiting for transfers between devices: 892 us -> none  [the longest x5 744 us: orthonormal_pair(): full_one, full_two = lax.psum((result_one, result_two), 'dp')]
    psum x11 -> x0, blocking collectives: 247 us -> none  [the longest x6 143 us: sketch_round(): first, second = lax.psum((first, second), 'tensor')]
    pallas_call x0 -> x2, Pallas kernels: none -> 171 us  [the longest x1 170 us: local(): pl.pallas_call(kernel, out_shape=(jax.ShapeDtypeStruct((R, n_narrow), bf1...]
    dot_general x34 -> x0, matrix products: 67.8 us -> none  [the longest x12 21 us: contract(): lax.dot_general(panel, rows, (((1,), (1,)), ((), ())), preferred_element_...]
    another operation x50 -> x0, other arithmetic: 66.9 us -> none  [the longest x30 36 us: normalize_rows(): lower = jnp.linalg.cholesky(gram)]
    another operation x10 -> x0, matrix products: 18.8 us -> none  [normalize_rows(): jax.scipy.linalg.solve_triangular(lower, panel, lower=True)]
  transfers between devices with their start and end apart: 6 -> 0, of which waited for: 6 -> 0; matrix products, arithmetic and copies ran while one was open for 0% -> 0% of each run, Pallas kernels for 0% -> 0%
where the time goes in v2:
time: 176 us
  Pallas kernels  171 us (97%)
  local copies, waits for them, and re-layouts  3.85 us (2%)
    pallas_call x1, Pallas kernels, local(): pl.pallas_call(kernel, out_shape=(jax.ShapeDtypeStruct((R, n_narrow), bf1...  170 us
    unnamed x8, local copies, waits for them, and re-layouts  3.85 us

profile of v2, /device:TPU:2, one launch (start us, length us, event | category | flops | bytes accessed | tf_op | source)
XLA Modules:
  0.0 175.6 jit_solution(14712532788648616809)
XLA Ops:
  0.6 169.7 %shard_map.93 = (bf16[32,2048]{1,0:T(8,128)(2,1)}, bf16[32,4,16,128]{3,2,1,0:T(8,128)(2,1)}, bf16[32,6656]{1,0:T(8,128)(2,1)}, bf16[32,16,128]{2,1,0:T(8,128)(2,1)}) custom-call(bf16[256,2048]{1,0:T(8,128)(2,1)} %x_in.1, bf16[256,6656]{1,0:T(8,128)(2,1)} %grad_up.1, bf16[256,6656]{1,0:T(8,128)(2,1)} %hidden_act.1, bf16[256,2048]{1,0:T(8,128)(2,1)} %grad_down.1, ...), custom_call_target="tpu_custom_call" | custom-call | tf_op jit(solution)/shard_map/pallas_call | solution.py:478
  170.3 0.0 copy-start
  170.4 1.0 copy-done
  171.4 0.0 copy-start.1
  171.4 1.0 copy-done.1
  172.4 0.0 copy-start.2
  172.4 0.9 copy-done.2
  173.3 0.0 copy-start.3
  173.3 0.9 copy-done.3
  174.2 1.4 shard_map.94
Async XLA Ops:
  170.3 1.0 copy-start
  171.4 1.0 copy-start.1
  172.4 0.9 copy-start.2
  173.3 0.9 copy-start.3

commit v3 on v2

--- a/solution.py
+++ b/solution.py
@@ -55,6 +55,15 @@
     return (work * scale)[:, R : 2 * R]
 
 
+def place(t, span, k):
+    row = min(t // span, NY - 1)
+    if t % span or row == 0 or t // span > row:
+        return row, t - span * row
+    if isinstance(k, int):
+        return (row - 1, span) if row > k else (row, 0)
+    return jnp.where(row > k, row - 1, row), jnp.where(row > k, span, 0)
+
+
 def settle(ref, sem):
     pltpu.make_async_copy(ref, ref, sem).wait()
 
@@ -65,9 +74,10 @@
     x_v, gu_v, h_v, gd_v, sk_wide, sk_narrow, qn_v, qw_v,
     up_wide, up_narrow, dn_wide, dn_narrow,
     ysend, yrecv, zown, zsend, zrecv, nsend, nrecv,
-    us, uc, ux, kparts, kbuf,
+    ux, kparts, kbuf,
     in_sem, out_sem, ys_sem, yr_sem, zs_sem, zr_sem, ag_sem, agz_sem, agy_sem,
-    ns_sem, nr_sem, nag_sem, nagr_sem, ks_sem, kr_sem, ucs_sem, ucr_sem, uxs_sem, uxr_sem,
+    ns_sem, nr_sem, nag_sem, nagr_sem, ks_sem, kr_sem, uxs_sem, uxr_sem,
+    ysx_sem, yx_sem, zsx_sem, zx_sem, agx_sem, agzs_sem, agzx_sem, agyx_sem,
 ):
     dp = lax.axis_index("dp")
     me_t = lax.axis_index("tensor")
@@ -129,14 +139,17 @@
 
     pl.semaphore_wait(barrier, len(peers))
 
+    def core_part(yy, kk):
+        return pl.ds(jnp.where(yy > kk, 1, 0), span)
+
+    last_part = pl.ds(span, 1)
+
     def wide_group(panel, i, kk):
         out = []
         for t in range(tiles):
-            yy = min(t // span, NY - 1)
+            yy, n = place(t, span, kk)
             out.append(
-                jnp.concatenate(
-                    [panel[i, (2 * kk + h) * NY + yy, t - span * yy] for h in range(2)], axis=0
-                )
+                jnp.concatenate([panel[i, (2 * kk + h) * NY + yy, n] for h in range(2)], axis=0)
             )
         return jnp.concatenate(out, axis=1)
 
@@ -156,9 +169,11 @@
         for o in (1, 2, 3, 4, 5, 6, 7):
             send(mine, mine, ks_sem.at[cp], kr_sem.at[cp, d], dev_t((me_t + o) % NT))
 
-    def send_core(cp, d, total):
-        us[cp, d] = total
-        send(us.at[cp, d], uc.at[cp, d], ucs_sem.at[cp], ucr_sem.at[cp, d], dev_t(x * NC + 1 - c))
+    def send_sums(cp, d, total):
+        ux[cp, d, me_t] = total.astype(jnp.bfloat16)
+        mine = ux.at[cp, d, me_t]
+        for o in (4, 3, 5, 2, 6, 1, 7):
+            send(mine, mine, uxs_sem.at[cp], uxr_sem.at[cp, d], dev_t((me_t + o) % NT))
 
     def past_sends(cp, d):
         @pl.when(d > 0)
@@ -167,20 +182,34 @@
 
     def last_tensor(cp):
         settle(kbuf.at[cp, 0, pl.ds(0, NT - 1)], ks_sem.at[cp])
-        settle(us.at[cp, 0], ucs_sem.at[cp])
-        settle(ux.at[cp, 0, pl.ds(0, (NX - 1) * NC)], uxs_sem.at[cp])
+        settle(ux.at[cp, 0, pl.ds(0, NT - 1)], uxs_sem.at[cp])
 
     def last_wide(w):
-        settle(ysend.at[w, 0, pl.ds(0, NZ * (NY - 1))], ys_sem.at[w])
-        settle(zsend.at[w, 0, pl.ds(0, NZ - 1)], zs_sem.at[w])
-        settle(up_wide.at[0, pl.ds(0, SLOTS - 1)], ag_sem.at[w])
+        settle(ysend.at[w, 0, pl.ds(0, NZ * (NY - 1)), pl.ds(0, span)], ys_sem.at[w])
+        settle(ysend.at[w, 0, pl.ds(0, 2 * (GROUPS - 1)), last_part], ysx_sem.at[w])
+        settle(zsend.at[w, 0, pl.ds(0, NZ - 1), pl.ds(0, span)], zs_sem.at[w])
+        settle(up_wide.at[0, pl.ds(0, SLOTS - 1), pl.ds(0, span)], ag_sem.at[w])
+        settle(up_wide.at[0, pl.ds(0, 2 * (NY - 1)), last_part], agx_sem.at[w])
+        for h in range(2):
+
+            @pl.when(z != 2 * y + h)
+            def _():
+                settle(zsend.at[w, 0, h, last_part], zsx_sem.at[w, h])
+
+        @pl.when(z // 2 == y)
+        def _():
+            settle(up_wide.at[0, pl.ds(0, NZ - 1), last_part], agzs_sem.at[w])
 
     def last_narrow(w):
         settle(nsend.at[w, 0, pl.ds(0, SLOTS - 1)], ns_sem.at[w])
         settle(up_narrow.at[0, pl.ds(0, SLOTS - 1)], nag_sem.at[w])
 
     def wait_wide(w, kk):
-        settle(up_wide.at[0, pl.ds(0, 2 * (NY - 1))], agy_sem.at[w, kk])
+        settle(up_wide.at[0, pl.ds(0, 2 * (NY - 1)), pl.ds(0, span)], agy_sem.at[w, kk])
+
+        @pl.when(kk != y)
+        def _():
+            settle(up_wide.at[0, pl.ds(0, 2), last_part], agyx_sem.at[w, kk])
 
     def wait_narrow(w):
         settle(up_narrow.at[0, pl.ds(0, SLOTS - 1)], nagr_sem.at[w])
@@ -204,7 +233,7 @@
                 send_gram(cp, d, ((kparts[0] + kparts[1]) + kparts[2]) + kparts[3])
             at = pl.ds(pl.multiple_of(kk * cols, LANES), cols)
             total = total + nt_dot(part, rows[:, at])
-        send_core(cp, d, total)
+        send_sums(cp, d, total)
 
     def sums_narrow(cp, d, panel, w, rows, fresh):
         past_sends(cp, d)
@@ -218,17 +247,7 @@
 
         part = narrow_all(panel, d)
         send_gram(cp, d, nt_dot(part, part))
-        send_core(cp, d, nt_dot(part, rows[...]))
-
-    def over_chip(cp, d):
-        settle(uc.at[cp, d], ucr_sem.at[cp, d])
-        total = (us[cp, d] + uc[cp, d]).astype(jnp.bfloat16)
-        for h in range(2):
-            ux[cp, d, x * NC + h] = total[HALF * h : HALF * h + HALF]
-        mine = ux.at[cp, d, me_t]
-        for o in (2, 1, 3):
-            for cc in range(NC):
-                send(mine, mine, uxs_sem.at[cp], uxr_sem.at[cp, d], dev_t(((x + o) % NX) * NC + cc))
+        send_sums(cp, d, nt_dot(part, rows[...]))
 
     def tokens_done(cp, d, first):
         settle(kbuf.at[cp, d, pl.ds(0, NT - 1)], kr_sem.at[cp, d])
@@ -242,14 +261,10 @@
             col = lax.broadcasted_iota(jnp.int32, (R, R), 1)
             identity = jnp.where(row == col, 1.0, 0.0)
             inverse = jnp.where(jnp.full((R, R), d) == 0, identity, inverse)
-        settle(ux.at[cp, d, pl.ds(0, (NX - 1) * NC)], uxr_sem.at[cp, d])
-        halves = []
-        for h in range(2):
-            total = ux[cp, d, h].astype(jnp.float32)
-            for xx in range(1, NX):
-                total = total + ux[cp, d, xx * NC + h].astype(jnp.float32)
-            halves.append(total)
-        total = jnp.concatenate(halves, axis=0)
+        settle(ux.at[cp, d, pl.ds(0, NT - 1)], uxr_sem.at[cp, d])
+        total = ux[cp, d, 0].astype(jnp.float32)
+        for t in range(1, NT):
+            total = total + ux[cp, d, t].astype(jnp.float32)
         return inverse, nn_dot(inverse, total, lax.Precision.HIGHEST).astype(jnp.bfloat16)
 
     def scatter_wide(w, d, tok, rows):
@@ -272,47 +287,97 @@
                 zd = 2 * kk + h
                 for q in (2, 1, 3):
                     yd = (y + q) % NY
+                    part = core_part(yd, kk)
                     send(
-                        ysend.at[w, d, zd * NY + yd], yrecv.at[w, d, zd, q - 1],
+                        ysend.at[w, d, zd * NY + yd, part], yrecv.at[w, d, zd, q - 1, part],
                         ys_sem.at[w], yr_sem.at[w, zd], dev_dp(z, yd),
+                    )
+
+            @pl.when(kk != y)
+            def _():
+                for h in range(2):
+                    zd = 2 * kk + h
+                    q = (kk + NY - y) % NY
+                    send(
+                        ysend.at[w, d, zd * NY + kk, last_part],
+                        yrecv.at[w, d, zd, q - 1, last_part],
+                        ysx_sem.at[w], yx_sem.at[w, h], dev_dp(z, kk),
                     )
 
     def reduce_wide(w, d):
         for o in FAR + (0,):
             zd = (z + o) % NZ
-            settle(yrecv.at[w, d, zd], yr_sem.at[w, zd])
+            settle(yrecv.at[w, d, zd, pl.ds(0, NY - 1), pl.ds(0, span)], yr_sem.at[w, zd])
+
+            @pl.when(zd // 2 == y)
+            def _():
+                settle(yrecv.at[w, d, zd, pl.ds(0, NY - 1), last_part], yx_sem.at[w, zd % 2])
+
             total = ysend[w, d, zd * NY + y].astype(jnp.float32)
             for q in range(NY - 1):
                 total = total + yrecv[w, d, zd, q].astype(jnp.float32)
             if o:
                 zsend[w, d, zd] = total.astype(jnp.bfloat16)
+                part = core_part(y, zd // 2)
                 send(
-                    zsend.at[w, d, zd], zrecv.at[w, d, o - 1],
+                    zsend.at[w, d, zd, part], zrecv.at[w, d, o - 1, part],
                     zs_sem.at[w], zr_sem.at[w], dev_dp(zd, y),
                 )
+
+                @pl.when(zd // 2 == y)
+                def _():
+                    send(
+                        zsend.at[w, d, zd, last_part], zrecv.at[w, d, o - 1, last_part],
+                        zsx_sem.at[w, zd % 2], zx_sem.at[w], dev_dp(zd, y),
+                    )
+
             else:
                 zown[w] = total
 
     def to_y(w, panel, i, zs):
-        piece = panel.at[i, zs * NY + y]
+        s = zs * NY + y
+        piece = panel.at[i, s, core_part(y, zs // 2)]
         for q in (2, 1, 3):
             send(piece, piece, ag_sem.at[w], agy_sem.at[w, zs // 2], dev_dp(z, (y + q) % NY))
 
+        @pl.when(zs // 2 == y)
+        def _():
+            last = panel.at[i, s, last_part]
+            for q in (2, 1, 3):
+                send(last, last, agx_sem.at[w], agyx_sem.at[w, zs // 2], dev_dp(z, (y + q) % NY))
+
     def gather_wide(w, d, panel, i):
-        settle(zrecv.at[w, d], zr_sem.at[w])
+        settle(zrecv.at[w, d, pl.ds(0, NZ - 1), pl.ds(0, span)], zr_sem.at[w])
+
+        @pl.when(z // 2 == y)
+        def _():
+            settle(zrecv.at[w, d, pl.ds(0, NZ - 1), last_part], zx_sem.at[w])
+
         total = zown[w]
         for q in range(NZ - 1):
             total = total + zrecv[w, d, q].astype(jnp.float32)
         panel[i, slot] = total.astype(jnp.bfloat16)
-        piece = panel.at[i, slot]
+        piece = panel.at[i, slot, core_part(y, z // 2)]
         for o in NEAR:
             send(piece, piece, ag_sem.at[w], agz_sem.at[w, o - 1], dev_dp((z + o) % NZ, y))
+
+        @pl.when(z // 2 == y)
+        def _():
+            last = panel.at[i, slot, last_part]
+            for o in NEAR:
+                send(last, last, agzs_sem.at[w], agzx_sem.at[w, o - 1], dev_dp((z + o) % NZ, y))
+
         to_y(w, panel, i, z)
 
-    def forward_wide(w, panel, i, offsets):
-        for o in offsets:
+    def forward_wide(w, panel, i):
+        for o in NEAR:
             zs = (z + NZ - o) % NZ
-            settle(panel.at[i, zs * NY + y], agz_sem.at[w, o - 1])
+            settle(panel.at[i, zs * NY + y, pl.ds(0, span)], agz_sem.at[w, o - 1])
+
+            @pl.when(zs // 2 == y)
+            def _():
+                settle(panel.at[i, zs * NY + y, last_part], agzx_sem.at[w, o - 1])
+
             to_y(w, panel, i, zs)
 
     def direct(src, dst, send_sem, recv_sem):
@@ -352,8 +417,6 @@
     def pair(d, _):
         sums_narrow(2, d, dn_narrow, 1, gd_v, False)
         sums_wide(0, d, up_wide, 0, gu_v, False)
-        over_chip(2, d)
-        over_chip(0, d)
 
         @pl.when(d == 0)
         def _():
@@ -367,10 +430,9 @@
         reduce_wide(1, d)
         gather_narrow(0, d, up_narrow, d)
         gather_wide(1, d, dn_wide, d)
+        forward_wide(1, dn_wide, d)
         sums_narrow(1, d, up_narrow, 0, x_v, True)
-        forward_wide(1, dn_wide, d, NEAR[:4])
-        over_chip(1, d)
-        forward_wide(1, dn_wide, d, NEAR[4:])
+        sums_wide(3, d, dn_wide, 1, h_v, True)
         inverse, tok = tokens_done(1, d, False)
         scatter_wide(0, d, tok, gu_v)
 
@@ -379,9 +441,6 @@
             qn_v[...] = orthonormal(inverse, narrow_all(up_narrow, d))
             pltpu.make_async_copy(qn_v, up_q, out_sem.at[0]).start()
 
-        sums_wide(3, d, dn_wide, 1, h_v, True)
-        over_chip(3, d)
-        reduce_wide(0, d)
         inverse, tok = tokens_done(3, d, False)
         scatter_narrow(1, d, tok, gd_v)
 
@@ -391,10 +450,10 @@
                 qw_v[:, k * cols : (k + 1) * cols] = orthonormal(inverse, wide_group(dn_wide, d, k))
             pltpu.make_async_copy(qw_v, down_q, out_sem.at[1]).start()
 
+        reduce_wide(0, d)
         gather_wide(0, d, up_wide, d + 1)
-        forward_wide(0, up_wide, d + 1, NEAR[:4])
         gather_narrow(1, d, dn_narrow, d + 1)
-        forward_wide(0, up_wide, d + 1, NEAR[4:])
+        forward_wide(0, up_wide, d + 1)
         return 0
 
     lax.fori_loop(0, PAIRS, pair, 0)
@@ -417,24 +476,45 @@
     up_out.wait()
 
 
-def finish(scales, up_q, up_img, down_q, down_img, up_a, up_b, down_a, down_b):
+def finish(scales, up_q, up_img, down_q, down_img, up_a, up_b, down_a, down_b, uq, ui, dq, di, ua, ub, da, db, sem):
     up_scale, down_scale, scale = scales
-    up_a[...] = up_q[...].astype(jnp.float32) * up_scale
-    down_a[...] = down_q[...].astype(jnp.float32) * down_scale
-    tiles = up_b.shape[1] // LANES // GROUPS
+    loads = [
+        pltpu.make_async_copy(src, dst, sem.at[i])
+        for i, (src, dst) in enumerate(((up_q, uq), (down_q, dq), (down_img, di), (up_img, ui)))
+    ]
+    for load in loads:
+        load.start()
+    stores = [
+        pltpu.make_async_copy(src, dst, sem.at[4 + i])
+        for i, (src, dst) in enumerate(((ua, up_a), (da, down_a), (db, down_b), (ub, up_b)))
+    ]
+    loads[0].wait()
+    ua[...] = uq[...].astype(jnp.float32) * up_scale
+    stores[0].start()
+    loads[1].wait()
+    da[...] = dq[...].astype(jnp.float32) * down_scale
+    stores[1].start()
+    tiles = ub.shape[1] // LANES // GROUPS
     span = tiles // NY
+    loads[2].wait()
     for k in range(GROUPS):
         for h in range(2):
-            rows = slice(HALF * h, HALF * h + HALF)
-            for t in range(tiles):
-                yy = min(t // span, NY - 1)
-                lo = (k * tiles + t) * LANES
-                piece = up_img[(2 * k + h) * NY + yy, t - span * yy]
-                up_b[rows, lo : lo + LANES] = piece.astype(jnp.float32) * scale
             for yy in range(NY):
                 lo = (k * NY + yy) * LANES
-                piece = down_img[(2 * k + h) * NY + yy]
-                down_b[rows, lo : lo + LANES] = piece.astype(jnp.float32) * scale
+                piece = di[(2 * k + h) * NY + yy]
+                db[HALF * h : HALF * h + HALF, lo : lo + LANES] = piece.astype(jnp.float32) * scale
+    stores[2].start()
+    loads[3].wait()
+    for k in range(GROUPS):
+        for h in range(2):
+            for t in range(tiles):
+                yy, n = place(t, span, k)
+                lo = (k * tiles + t) * LANES
+                piece = ui[(2 * k + h) * NY + yy, n]
+                ub[HALF * h : HALF * h + HALF, lo : lo + LANES] = piece.astype(jnp.float32) * scale
+    stores[3].start()
+    for store in stores:
+        store.wait()
 
 
 def local(x_in, grad_up, hidden_act, grad_down, sketch_up, sketch_down):
@@ -465,15 +545,15 @@
         vmem((2, PAIRS, NZ - 1) + piece, bf16),
         vmem((2, PAIRS, SLOTS) + tail, bf16),
         vmem((2, PAIRS, SLOTS) + tail, bf16),
-        vmem((4, PAIRS, R, tokens), f32),
-        vmem((4, PAIRS, R, tokens), f32),
-        vmem((4, PAIRS, NT, HALF, tokens), bf16),
+        vmem((4, PAIRS, NT, R, tokens), bf16),
         vmem((GROUPS, R, R), f32),
         vmem((4, PAIRS, NT, 8, LANES), f32),
         dma((6,)), dma((4,)), dma((2,)), dma((2, NZ)), dma((2,)), dma((2,)),
         dma((2,)), dma((2, NZ - 1)), dma((2, GROUPS)),
         dma((2,)), dma((2,)), dma((2,)), dma((2,)),
-        dma((4,)), dma((4, PAIRS)), dma((4,)), dma((4, PAIRS)), dma((4,)), dma((4, PAIRS)),
+        dma((4,)), dma((4, PAIRS)), dma((4,)), dma((4, PAIRS)),
+        dma((2,)), dma((2, 2)), dma((2, 2)), dma((2,)),
+        dma((2,)), dma((2,)), dma((2, NZ - 1)), dma((2, GROUPS)),
     ]
     panels = pl.pallas_call(
         kernel,
@@ -496,17 +576,19 @@
         math.sqrt(n_wide * width),
         1.0 / math.sqrt(tokens * lax.axis_size("dp")),
     )
+    outs = (
+        jax.ShapeDtypeStruct((R, n_narrow), f32),
+        jax.ShapeDtypeStruct((R, n_wide), f32),
+        jax.ShapeDtypeStruct((R, n_wide), f32),
+        jax.ShapeDtypeStruct((R, n_narrow), f32),
+    )
     return pl.pallas_call(
         functools.partial(finish, scales),
-        out_shape=(
-            jax.ShapeDtypeStruct((R, n_narrow), f32),
-            jax.ShapeDtypeStruct((R, n_wide), f32),
-            jax.ShapeDtypeStruct((R, n_wide), f32),
-            jax.ShapeDtypeStruct((R, n_narrow), f32),
-        ),
-        in_specs=[pl.BlockSpec(memory_space=pltpu.VMEM)] * 4,
-        out_specs=[pl.BlockSpec(memory_space=pltpu.VMEM)] * 4,
-        compiler_params=pltpu.CompilerParams(vmem_limit_bytes=16 * 2**20),
+        out_shape=outs,
+        in_specs=[pl.BlockSpec(memory_space=pl.ANY)] * 4,
+        out_specs=[pl.BlockSpec(memory_space=pl.ANY)] * 4,
+        scratch_shapes=[vmem(a.shape, a.dtype) for a in tuple(panels) + outs] + [dma((8,))],
+        compiler_params=pltpu.CompilerParams(vmem_limit_bytes=56 * 2**20),
     )(*panels)
 
 

time: 176 us -> 167 us (0.949)
  Pallas kernels: 171 us -> 167 us
  local copies, waits for them, and re-layouts: 3.85 us -> 0 us
    pallas_call x1, Pallas kernels: 170 us -> 164 us  [local(): pl.pallas_call(kernel, out_shape=(jax.ShapeDtypeStruct((R, n_narrow), bf1...]
    unnamed x8 -> x0, local copies, waits for them, and re-layouts: 3.85 us -> none
where the time goes in v3:
time: 167 us
  Pallas kernels  167 us (100%)
    pallas_call x1, Pallas kernels, local(): pl.pallas_call(kernel, out_shape=(jax.ShapeDtypeStruct((R, n_narrow), bf1...  164 us

profile of v3, /device:TPU:2, one launch (start us, length us, event | category | flops | bytes accessed | tf_op | source)
XLA Modules:
  0.0 167.3 jit_solution(10815809348019048419)
XLA Ops:
  0.6 164.2 %shard_map.93 = (bf16[32,2048]{1,0:T(8,128)(2,1)}, bf16[32,4,16,128]{3,2,1,0:T(8,128)(2,1)}, bf16[32,6656]{1,0:T(8,128)(2,1)}, bf16[32,16,128]{2,1,0:T(8,128)(2,1)}) custom-call(bf16[256,2048]{1,0:T(8,128)(2,1)} %x_in.1, bf16[256,6656]{1,0:T(8,128)(2,1)} %grad_up.1, bf16[256,6656]{1,0:T(8,128)(2,1)} %hidden_act.1, bf16[256,2048]{1,0:T(8,128)(2,1)} %grad_down.1, ...), custom_call_target="tpu_custom_call" | custom-call | tf_op jit(solution)/shard_map/pallas_call | solution.py:558
  164.8 2.5 %shard_map.94 = (f32[32,2048]{1,0:T(8,128)}, f32[32,6656]{1,0:T(8,128)}, f32[32,6656]{1,0:T(8,128)}, f32[32,2048]{1,0:T(8,128)}) custom-call(bf16[32,2048]{1,0:T(8,128)(2,1)} %get-tuple-element.8.up_q, bf16[32,4,16,128]{3,2,1,0:T(8,128)(2,1)} %get-tuple-element.9.up_img, bf16[32,6656]{1,0:T(8,128)(2,1)} %get-tuple-element.10.down_q, ...), custom_call_target="tpu_custom_call" | custom-call | tf_op jit(solution)/shard_map/pallas_call | solution.py:585

commit v4 on v3

--- a/solution.py
+++ b/solution.py
@@ -137,8 +137,6 @@
                 lo = (k * NY + yy) * LANES
                 dn_narrow[0, s] = sk_narrow[rows, lo : lo + LANES]
 
-    pl.semaphore_wait(barrier, len(peers))
-
     def core_part(yy, kk):
         return pl.ds(jnp.where(yy > kk, 1, 0), span)
 
@@ -162,23 +160,19 @@
             )
         return jnp.concatenate(out, axis=1)
 
-    def send_gram(cp, d, gram):
+    def keep_gram(cp, d, gram):
         packed = jnp.concatenate([gram[8 * j : 8 * j + 8, :] for j in range(R // 8)], axis=1)
         kbuf[cp, d, me_t] = packed
+
+    def send_gram(cp, d):
         mine = kbuf.at[cp, d, me_t]
         for o in (1, 2, 3, 4, 5, 6, 7):
             send(mine, mine, ks_sem.at[cp], kr_sem.at[cp, d], dev_t((me_t + o) % NT))
 
-    def send_sums(cp, d, total):
-        ux[cp, d, me_t] = total.astype(jnp.bfloat16)
+    def send_sums(cp, d):
         mine = ux.at[cp, d, me_t]
         for o in (4, 3, 5, 2, 6, 1, 7):
             send(mine, mine, uxs_sem.at[cp], uxr_sem.at[cp, d], dev_t((me_t + o) % NT))
-
-    def past_sends(cp, d):
-        @pl.when(d > 0)
-        def _():
-            last_tensor(cp)
 
     def last_tensor(cp):
         settle(kbuf.at[cp, 0, pl.ds(0, NT - 1)], ks_sem.at[cp])
@@ -214,40 +208,34 @@
     def wait_narrow(w):
         settle(up_narrow.at[0, pl.ds(0, SLOTS - 1)], nagr_sem.at[w])
 
-    def sums_wide(cp, d, panel, w, rows, fresh):
-        past_sends(cp, d)
+    def sums_wide(cp, d, panel, w, rows, start=False):
         total = jnp.zeros((R, tokens), jnp.float32)
         for n, o in enumerate((0, 1, 3, 2)):
             kk = (z // 2 + o) % GROUPS
-            if fresh:
+            if not start:
                 wait_wide(w, kk)
-            else:
-
-                @pl.when(d > 0)
-                def _():
-                    wait_wide(w, kk)
-
             part = wide_group(panel, d, kk)
             kparts[kk] = nt_dot(part, part)
             if n == GROUPS - 1:
-                send_gram(cp, d, ((kparts[0] + kparts[1]) + kparts[2]) + kparts[3])
+                keep_gram(cp, d, ((kparts[0] + kparts[1]) + kparts[2]) + kparts[3])
+                if not start:
+                    send_gram(cp, d)
             at = pl.ds(pl.multiple_of(kk * cols, LANES), cols)
             total = total + nt_dot(part, rows[:, at])
-        send_sums(cp, d, total)
-
-    def sums_narrow(cp, d, panel, w, rows, fresh):
-        past_sends(cp, d)
-        if fresh:
+        ux[cp, d, me_t] = total.astype(jnp.bfloat16)
+        if not start:
+            send_sums(cp, d)
+
+    def sums_narrow(cp, d, panel, w, rows, start=False):
+        if not start:
             wait_narrow(w)
-        else:
-
-            @pl.when(d > 0)
-            def _():
-                wait_narrow(w)
-
         part = narrow_all(panel, d)
-        send_gram(cp, d, nt_dot(part, part))
-        send_sums(cp, d, nt_dot(part, rows[...]))
+        keep_gram(cp, d, nt_dot(part, part))
+        if not start:
+            send_gram(cp, d)
+        ux[cp, d, me_t] = nt_dot(part, rows[...]).astype(jnp.bfloat16)
+        if not start:
+            send_sums(cp, d)
 
     def tokens_done(cp, d, first):
         settle(kbuf.at[cp, d, pl.ds(0, NT - 1)], kr_sem.at[cp, d])
@@ -415,9 +403,6 @@
         return nn_dot(inverse, part.astype(jnp.float32), lax.Precision.HIGHEST).astype(jnp.bfloat16)
 
     def pair(d, _):
-        sums_narrow(2, d, dn_narrow, 1, gd_v, False)
-        sums_wide(0, d, up_wide, 0, gu_v, False)
-
         @pl.when(d == 0)
         def _():
             loads[4].wait()
@@ -431,8 +416,14 @@
         gather_narrow(0, d, up_narrow, d)
         gather_wide(1, d, dn_wide, d)
         forward_wide(1, dn_wide, d)
-        sums_narrow(1, d, up_narrow, 0, x_v, True)
-        sums_wide(3, d, dn_wide, 1, h_v, True)
+
+        @pl.when(d > 0)
+        def _():
+            last_tensor(1)
+            last_tensor(3)
+
+        sums_narrow(1, d, up_narrow, 0, x_v)
+        sums_wide(3, d, dn_wide, 1, h_v)
         inverse, tok = tokens_done(1, d, False)
         scatter_wide(0, d, tok, gu_v)
 
@@ -454,8 +445,22 @@
         gather_wide(0, d, up_wide, d + 1)
         gather_narrow(1, d, dn_narrow, d + 1)
         forward_wide(0, up_wide, d + 1)
+
+        @pl.when(d + 1 < PAIRS)
+        def _():
+            last_tensor(2)
+            last_tensor(0)
+            sums_narrow(2, d + 1, dn_narrow, 1, gd_v)
+            sums_wide(0, d + 1, up_wide, 0, gu_v)
+
         return 0
 
+    sums_narrow(2, 0, dn_narrow, 1, gd_v, True)
+    sums_wide(0, 0, up_wide, 0, gu_v, True)
+    pl.semaphore_wait(barrier, len(peers))
+    for cp in (2, 0):
+        send_gram(cp, 0)
+        send_sums(cp, 0)
     lax.fori_loop(0, PAIRS, pair, 0)
 
     wait_narrow(1)

time: 167 us -> 167 us (level)
  Pallas kernels: 167 us -> 165 us
where the time goes in v4:
time: 167 us; the launch traced here: 166 us
  Pallas kernels  165 us (99%)
    pallas_call x1, Pallas kernels, local(): pl.pallas_call(kernel, out_shape=(jax.ShapeDtypeStruct((R, n_narrow), bf1...  163 us

profile of v4, /device:TPU:2, one launch (start us, length us, event | category | flops | bytes accessed | tf_op | source)
XLA Modules:
  0.0 166.1 jit_solution(13509195110730822507)
XLA Ops:
  0.6 163.0 %shard_map.93 = (bf16[32,2048]{1,0:T(8,128)(2,1)}, bf16[32,4,16,128]{3,2,1,0:T(8,128)(2,1)}, bf16[32,6656]{1,0:T(8,128)(2,1)}, bf16[32,16,128]{2,1,0:T(8,128)(2,1)}) custom-call(bf16[256,2048]{1,0:T(8,128)(2,1)} %x_in.1, bf16[256,6656]{1,0:T(8,128)(2,1)} %grad_up.1, bf16[256,6656]{1,0:T(8,128)(2,1)} %hidden_act.1, bf16[256,2048]{1,0:T(8,128)(2,1)} %grad_down.1, ...), custom_call_target="tpu_custom_call" | custom-call | tf_op jit(solution)/shard_map/pallas_call | solution.py:563
  163.6 2.5 %shard_map.94 = (f32[32,2048]{1,0:T(8,128)}, f32[32,6656]{1,0:T(8,128)}, f32[32,6656]{1,0:T(8,128)}, f32[32,2048]{1,0:T(8,128)}) custom-call(bf16[32,2048]{1,0:T(8,128)(2,1)} %get-tuple-element.8.up_q, bf16[32,4,16,128]{3,2,1,0:T(8,128)(2,1)} %get-tuple-element.9.up_img, bf16[32,6656]{1,0:T(8,128)(2,1)} %get-tuple-element.10.down_q, ...), custom_call_target="tpu_custom_call" | custom-call | tf_op jit(solution)/shard_map/pallas_call | solution.py:590

commit v5 on v4

--- a/solution.py
+++ b/solution.py
@@ -175,7 +175,13 @@
             send(mine, mine, uxs_sem.at[cp], uxr_sem.at[cp, d], dev_t((me_t + o) % NT))
 
     def last_tensor(cp):
+        settle_gram(cp)
+        settle_sums(cp)
+
+    def settle_gram(cp):
         settle(kbuf.at[cp, 0, pl.ds(0, NT - 1)], ks_sem.at[cp])
+
+    def settle_sums(cp):
         settle(ux.at[cp, 0, pl.ds(0, NT - 1)], uxs_sem.at[cp])
 
     def last_wide(w):
@@ -215,10 +221,10 @@
             if not start:
                 wait_wide(w, kk)
             part = wide_group(panel, d, kk)
-            kparts[kk] = nt_dot(part, part)
-            if n == GROUPS - 1:
-                keep_gram(cp, d, ((kparts[0] + kparts[1]) + kparts[2]) + kparts[3])
-                if not start:
+            if not start:
+                kparts[kk] = nt_dot(part, part)
+                if n == GROUPS - 1:
+                    keep_gram(cp, d, ((kparts[0] + kparts[1]) + kparts[2]) + kparts[3])
                     send_gram(cp, d)
             at = pl.ds(pl.multiple_of(kk * cols, LANES), cols)
             total = total + nt_dot(part, rows[:, at])
@@ -230,15 +236,18 @@
         if not start:
             wait_narrow(w)
         part = narrow_all(panel, d)
-        keep_gram(cp, d, nt_dot(part, part))
         if not start:
+            keep_gram(cp, d, nt_dot(part, part))
             send_gram(cp, d)
         ux[cp, d, me_t] = nt_dot(part, rows[...]).astype(jnp.bfloat16)
         if not start:
             send_sums(cp, d)
 
     def tokens_done(cp, d, first):
-        settle(kbuf.at[cp, d, pl.ds(0, NT - 1)], kr_sem.at[cp, d])
+        @pl.when(d > 0 if first else d >= 0)
+        def _():
+            settle(kbuf.at[cp, d, pl.ds(0, NT - 1)], kr_sem.at[cp, d])
+
         packed = kbuf[cp, d, 0]
         for t in range(1, NT):
             packed = packed + kbuf[cp, d, t]
@@ -448,8 +457,13 @@
 
         @pl.when(d + 1 < PAIRS)
         def _():
-            last_tensor(2)
-            last_tensor(0)
+            for cp in (2, 0):
+                settle_sums(cp)
+
+                @pl.when(d > 0)
+                def _():
+                    settle_gram(cp)
+
             sums_narrow(2, d + 1, dn_narrow, 1, gd_v)
             sums_wide(0, d + 1, up_wide, 0, gu_v)
 
@@ -459,7 +473,6 @@
     sums_wide(0, 0, up_wide, 0, gu_v, True)
     pl.semaphore_wait(barrier, len(peers))
     for cp in (2, 0):
-        send_gram(cp, 0)
         send_sums(cp, 0)
     lax.fori_loop(0, PAIRS, pair, 0)
 

time: 167 us -> 167 us (level)
  no operation moved by 1% of the time
where the time goes in v5:
time: 167 us; the launch traced here: 166 us
  Pallas kernels  166 us (99%)
    pallas_call x1, Pallas kernels, local(): pl.pallas_call(kernel, out_shape=(jax.ShapeDtypeStruct((R, n_narrow), bf1...  163 us

profile of v5, /device:TPU:2, one launch (start us, length us, event | category | flops | bytes accessed | tf_op | source)
XLA Modules:
  0.0 166.3 jit_solution(2453602845247558921)
XLA Ops:
  0.6 163.1 %shard_map.93 = (bf16[32,2048]{1,0:T(8,128)(2,1)}, bf16[32,4,16,128]{3,2,1,0:T(8,128)(2,1)}, bf16[32,6656]{1,0:T(8,128)(2,1)}, bf16[32,16,128]{2,1,0:T(8,128)(2,1)}) custom-call(bf16[256,2048]{1,0:T(8,128)(2,1)} %x_in.1, bf16[256,6656]{1,0:T(8,128)(2,1)} %grad_up.1, bf16[256,6656]{1,0:T(8,128)(2,1)} %hidden_act.1, bf16[256,2048]{1,0:T(8,128)(2,1)} %grad_down.1, ...), custom_call_target="tpu_custom_call" | custom-call | tf_op jit(solution)/shard_map/pallas_call | solution.py:576
  163.8 2.5 %shard_map.94 = (f32[32,2048]{1,0:T(8,128)}, f32[32,6656]{1,0:T(8,128)}, f32[32,6656]{1,0:T(8,128)}, f32[32,2048]{1,0:T(8,128)}) custom-call(bf16[32,2048]{1,0:T(8,128)(2,1)} %get-tuple-element.8.up_q, bf16[32,4,16,128]{3,2,1,0:T(8,128)(2,1)} %get-tuple-element.9.up_img, bf16[32,6656]{1,0:T(8,128)(2,1)} %get-tuple-element.10.down_q, ...), custom_call_target="tpu_custom_call" | custom-call | tf_op jit(solution)/shard_map/pallas_call | solution.py:603
